TPU v7x, 32 devices: a whole 2x2x4 slice. The times are simulated.
32 devices in a mesh: gx: 8 (over z, x), gy: 4 (over y, core).
Axes of the slice: x: 2, y: 2, z: 4, core: 2. Of those that a mesh axis runs over, the one named last changes fastest.
Arguments:
- polar: float32 [512, 3072], P('gx', 'gy'), may hold values from -3.140625 to 3.140625
- azimuth: float32 [512, 3072], P('gx', 'gy'), may hold values from -3.140625 to 3.140625
- grains: int32 [512, 3072], P('gx', 'gy'), may hold values from 0 to 255, as said below
- stiffness: float32 [256], replicated, may hold values from 0.5 to 2
- anisotropy: float32 [256], replicated, may hold values from 0.2 to 2
- axis_polar: float32 [256], replicated, may hold values from -3.140625 to 3.140625
- axis_azimuth: float32 [256], replicated, may hold values from -3.140625 to 3.140625
- applied_field: float32 [3], replicated, may hold values from -3 to 3
Outputs:
- moment: float32 [3, 512, 3072], P(None, 'gx', 'gy')
- spin_flip: float32 [512, 256], P(('gx', 'gy'))
- non_flip: float32 [512, 256], P(('gx', 'gy'))
Inputs may be any that keep to these rules, and one draw needn't show every extreme that they name: `grains`: grain label of each cell, a row of the grain tables.
All inputs are finite; a program needn't handle non-finite values.
Results may differ from a plain program's by a relative error of at most 0.0003.
Values sent between devices are 32-bit elements; how exact they have to be, the bound alone decides.
A program may use at most 128 MiB of HBM per device.

v0:
```python
import math

import jax
import jax.numpy as jnp
from jax import lax
from jax.sharding import PartitionSpec as P

NZ = 12
STEPS = 4


damping = 0.5
time_step = 0.12


def padded(block, sides, width):
    for axis, dim in sides:
        count = lax.axis_size(axis)
        forward = [(i, i + 1) for i in range(count - 1)]
        forward.append((count - 1, 0))
        backward = [(target, source) for source, target in forward]
        low = lax.ppermute(
            lax.slice_in_dim(block, block.shape[dim] - width, None, axis=dim), axis, forward
        )
        high = lax.ppermute(lax.slice_in_dim(block, 0, width, axis=dim), axis, backward)
        block = jnp.concatenate([low, block, high], axis=dim)
    return block


def couple(left, right):
    return 2.0 * left * right / (left + right)


def cross(first, second):
    return jnp.stack(
        [
            first[1] * second[2] - first[2] * second[1],
            first[2] * second[0] - first[0] * second[2],
            first[0] * second[1] - first[1] * second[0],
        ]
    )


def advance(
    center,
    plus_x,
    minus_x,
    plus_y,
    minus_y,
    weight,
    weight_px,
    weight_mx,
    weight_py,
    weight_my,
    strength,
    easy_axis,
    applied,
    depth,
):
    field = couple(weight, weight_px) * (plus_x - center) + couple(weight, weight_mx) * (
        minus_x - center
    )
    field = (
        field
        + couple(weight, weight_py) * (plus_y - center)
        + couple(weight, weight_my) * (minus_y - center)
    )
    columns = center.shape[-1]
    linked = (jnp.arange(1, columns, dtype=jnp.int32) % depth != 0).astype(jnp.float32)
    flux = couple(weight[:, 1:], weight[:, :-1]) * (center[..., 1:] - center[..., :-1]) * linked
    zeros = jnp.zeros_like(center[..., :1])
    field = (
        field + jnp.concatenate([flux, zeros], axis=-1) - jnp.concatenate([zeros, flux], axis=-1)
    )
    project = easy_axis[0] * center[0] + easy_axis[1] * center[1] + easy_axis[2] * center[2]
    field = field + strength * project * easy_axis + applied.reshape(3, 1, 1)
    torque = cross(center, field)
    damped = cross(center, torque)
    moved = center - time_step / (1.0 + damping * damping) * (torque + damping * damped)
    return moved / jnp.sqrt(moved[0] * moved[0] + moved[1] * moved[1] + moved[2] * moved[2])


def cross_sections(real_part, imag_part, wave_x, wave_y):
    squared = wave_x * wave_x + wave_y * wave_y
    inverse = 1.0 / jnp.sqrt(jnp.maximum(squared, 1.0))
    beam_stop = jnp.where(squared > 0.5, 1.0, 0.0).astype(real_part.dtype)
    unit_x = wave_x * inverse
    unit_y = wave_y * inverse
    pieces = []
    for part in (real_part, imag_part):
        along = unit_x * part[0] + unit_y * part[1]
        pieces.append((part[0] - unit_x * along, part[1] - unit_y * along, part[2]))
    non_flip = pieces[0][0] * pieces[0][0] + pieces[1][0] * pieces[1][0]
    spin_flip = (
        pieces[0][1] * pieces[0][1]
        + pieces[1][1] * pieces[1][1]
        + pieces[0][2] * pieces[0][2]
        + pieces[1][2] * pieces[1][2]
    )
    return (spin_flip * beam_stop, non_flip * beam_stop)


def lookup(grains, table_rows):
    count = table_rows.shape[1]
    labels_all = jnp.arange(count, dtype=jnp.int32)

    def one_row(labels):
        onehot = (labels_all[:, None] == labels[None, :]).astype(jnp.float32)
        return jnp.dot(table_rows, onehot, precision=lax.Precision.HIGHEST)

    values = lax.map(one_row, grains)
    return jnp.transpose(values, (1, 0, 2))


def signed_rows(counter, length):
    return jnp.where(counter < length // 2, counter, counter - length).astype(jnp.float32)


def kernel(first, second, length):
    phase = (first[:, None] * second[None, :] % length).astype(jnp.float32) * (
        2.0 * math.pi / length
    )
    return (jnp.cos(phase), jnp.sin(phase))


def shards(polar, azimuth, grains, stiffness, anisotropy, axis_polar, axis_azimuth, applied_field):
    depth = NZ
    width_x, columns = polar.shape
    width_y = columns // depth
    total_x = width_x * lax.axis_size("gx")
    total_y = width_y * lax.axis_size("gy")
    moment = jnp.stack(
        [jnp.sin(polar) * jnp.cos(azimuth), jnp.sin(polar) * jnp.sin(azimuth), jnp.cos(polar)]
    )
    table_rows = jnp.stack(
        [
            stiffness,
            anisotropy,
            jnp.sin(axis_polar) * jnp.cos(axis_azimuth),
            jnp.sin(axis_polar) * jnp.sin(axis_azimuth),
            jnp.cos(axis_polar),
        ],
        axis=0,
    )
    props = lookup(grains, table_rows)
    weight = props[0]
    strength = props[1]
    easy_axis = props[2:5]
    weight_xpad = padded(weight, (("gx", 0),), 1)
    weight_ypad = padded(weight, (("gy", 1),), depth)
    weight_px = weight_xpad[2:]
    weight_mx = weight_xpad[:-2]
    weight_py = weight_ypad[:, 2 * depth :]
    weight_my = weight_ypad[:, : -2 * depth]
    for turn_index in range(STEPS):
        padded_x = padded(moment, (("gx", 1),), 1)
        padded_y = padded(moment, (("gy", 2),), depth)
        moment = advance(
            moment,
            padded_x[:, 2:],
            padded_x[:, :-2],
            padded_y[:, :, 2 * depth :],
            padded_y[:, :, : -2 * depth],
            weight,
            weight_px,
            weight_mx,
            weight_py,
            weight_my,
            strength,
            easy_axis,
            applied_field,
            depth,
        )
    layer = jnp.sum(moment.reshape(3, width_x, width_y, depth), axis=3) / math.sqrt(depth)
    flat = jnp.transpose(layer, (1, 0, 2)).reshape(width_x, 3 * width_y)
    cell_x = lax.axis_index("gx") * width_x + jnp.arange(width_x, dtype=jnp.int32)
    waves = jnp.arange(width_x * lax.axis_size("gx"), dtype=jnp.int32)
    cosine, sine = kernel(waves, cell_x, total_x)
    partial_x = lax.psum_scatter(
        jnp.concatenate(
            [
                jnp.dot(cosine, flat, precision=lax.Precision.HIGHEST),
                -jnp.dot(sine, flat, precision=lax.Precision.HIGHEST),
            ],
            axis=1,
        ),
        "gx",
        scatter_dimension=0,
        tiled=True,
    )
    arranged = lax.all_to_all(
        partial_x.reshape(width_x, 6, width_y), "gy", split_axis=0, concat_axis=2, tiled=True
    )
    rows_here = arranged.shape[0]
    cells_y = jnp.arange(total_y, dtype=jnp.int32)
    cosine_y, sine_y = kernel(cells_y, cells_y, total_y)
    real_in = arranged[:, :3].reshape(rows_here * 3, total_y)
    imag_in = arranged[:, 3:].reshape(rows_here * 3, total_y)
    real_cos = jnp.dot(real_in, cosine_y, precision=lax.Precision.HIGHEST)
    real_sin = jnp.dot(real_in, sine_y, precision=lax.Precision.HIGHEST)
    imag_cos = jnp.dot(imag_in, cosine_y, precision=lax.Precision.HIGHEST)
    imag_sin = jnp.dot(imag_in, sine_y, precision=lax.Precision.HIGHEST)
    scale = math.sqrt(total_x * total_y)
    real_part = (
        jnp.transpose((real_cos + imag_sin).reshape(rows_here, 3, total_y), (1, 0, 2)) / scale
    )
    imag_part = (
        jnp.transpose((imag_cos - real_sin).reshape(rows_here, 3, total_y), (1, 0, 2)) / scale
    )
    row_waves = (
        lax.axis_index("gx") * width_x
        + lax.axis_index("gy") * rows_here
        + jnp.arange(rows_here, dtype=jnp.int32)
    )
    wave_x = signed_rows(row_waves, total_x)[:, None]
    wave_y = signed_rows(cells_y, total_y)[None, :]
    spin_flip, non_flip = cross_sections(real_part, imag_part, wave_x, wave_y)
    return (moment, spin_flip, non_flip)


def solution(mesh):
    in_specs = (P("gx", "gy"), P("gx", "gy"), P("gx", "gy"), P(), P(), P(), P(), P())
    out_specs = (P(None, "gx", "gy"), P(("gx", "gy"), None), P(("gx", "gy"), None))
    return jax.shard_map(shards, mesh=mesh, in_specs=in_specs, out_specs=out_specs, check_vma=False)
```

profile of v0, /device:TPU:0, one launch (start us, length us, event | category | flops | bytes accessed | tf_op | source)
XLA Modules:
  0.0 352.5 jit_solution(14508015744952796817)
XLA Ops:
  11.0 81.4 %while.11 = (s32[]{:T(128)}, f32[64,5,768]{2,0,1:T(8,128)S(1)}, s32[64,768]{1,0:T(8,128)}, f32[5,256]{1,0:T(8,128)S(1)}, s32[]{:T(128)}, /*index=5*/s32[]{:T(128)}) while((s32[]{:T(128)}, f32[64,5,768]{2,0,1:T(8,128)S(1)}, s32[64,768]{1,0:T(8,128)}, f32[5,256]{1,0:T(8,128)S(1)}, s32[]{:T(128)}, /*index=5*/s32[]{:T(128)}) %tuple.59), condition=%wide.region_1.2_spmd.clone, body=%wide.region_0.1_spmd.clone.sunk | while | flops 11993090 | bytes 91221 | solution.py:111
  94.5 5.6 %collective-permute-start = (f32[1,768]{1,0:T(1,128)S(1)}, f32[1,768]{1,0:T(1,128)S(1)}, u32[]{:S(2)}, u32[]{:S(2)}) collective-permute-start(f32[1,768]{1,0:T(1,128)S(1)} %get-tuple-element.72), channel_id=1, source_target_pairs={{4,0},{8,4},{12,8},{16,12},{20,16},{24,20},{28,24},{0,28},{5,1},{9... | collective-permute-start | bytes 9224 | tf_op jit(solution)/shard_map/ppermute | solution.py:25
  108.8 4.8 %collective-permute-start.1 = (f32[3,1,768]{2,1,0:T(1,128)S(1)}, f32[3,1,768]{2,1,0:T(1,128)S(1)}, u32[]{:S(2)}, u32[]{:S(2)}) collective-permute-start(f32[3,1,768]{2,1,0:T(1,128)S(1)} %get-tuple-element.86), channel_id=1, source_target_pairs={{4,0},{8,4},{12,8},{16,12},{20,16},{24,20},{28,24},{0,28},{5,1},{9... | collective-permute-start | bytes 27656 | tf_op jit(solution)/shard_map/ppermute | solution.py:25
  122.9 4.7 %collective-permute-start.8 = (f32[3,1,768]{2,1,0:T(1,128)}, f32[3,1,768]{2,1,0:T(1,128)}, u32[]{:S(2)}, u32[]{:S(2)}) collective-permute-start(f32[3,1,768]{2,1,0:T(1,128)} %get-tuple-element.82), channel_id=1, source_target_pairs={{4,0},{8,4},{12,8},{16,12},{20,16},{24,20},{28,24},{0,28},{5,1},{9... | collective-permute-start | bytes 27656 | tf_op jit(solution)/shard_map/ppermute | solution.py:25
  148.7 2.2 fusion.58
  158.0 4.7 %collective-permute-start.12 = (f32[3,1,768]{2,1,0:T(1,128)}, f32[3,1,768]{2,1,0:T(1,128)}, u32[]{:S(2)}, u32[]{:S(2)}) collective-permute-start(f32[3,1,768]{2,1,0:T(1,128)} %get-tuple-element.78), channel_id=1, source_target_pairs={{4,0},{8,4},{12,8},{16,12},{20,16},{24,20},{28,24},{0,28},{5,1},{9... | collective-permute-start | bytes 27656 | tf_op jit(solution)/shard_map/ppermute | solution.py:25
  167.2 1.9 copy.88
  173.8 1.9 copy.93
  180.0 1.9 copy.94
  183.7 2.2 fusion.41
  194.0 4.7 %collective-permute-start.16 = (f32[3,1,768]{2,1,0:T(1,128)}, f32[3,1,768]{2,1,0:T(1,128)}, u32[]{:S(2)}, u32[]{:S(2)}) collective-permute-start(f32[3,1,768]{2,1,0:T(1,128)} %get-tuple-element.74), channel_id=1, source_target_pairs={{4,0},{8,4},{12,8},{16,12},{20,16},{24,20},{28,24},{0,28},{5,1},{9... | collective-permute-start | bytes 27656 | tf_op jit(solution)/shard_map/ppermute | solution.py:25
  206.9 1.9 copy.96
  210.6 1.9 copy.106
  220.5 2.2 fusion.24
  225.7 1.9 copy.116
  229.5 3.0 fusion.91
  236.1 1.9 copy.109
  239.8 1.9 copy.119
  250.4 7.0 %fusion.13 = f32[3,64,64]{1,2,0:T(8,128)S(1)} fusion(f32[1,64,64,12]{1,3,2,0:T(8,128)} %copy.119, f32[1,64,64,12]{1,3,2,0:T(8,128)} %copy.118, f32[1,64,64,12]{1,3,2,0:T(8,128)} %copy.117, f32[1,64,64,12]{1,3,2,0:T(8,128)} %copy.113, f32[1,64,64,12]{1,3,2,0:T(8,128)} %copy.112, f32[1,64,64,12]{1,3,2,0:T(8,128)} %copy.111, f32[1,64,64,12]{1,3,2,0:T(8,128)} %copy.106, ...), kind=kLoop, calls=%fused_computation.24 | loop fusion | flops 5738496 | bytes 6144000 | tf_op jit(solution)/shard_map/reduce_sum | solution.py:174
  261.3 2.3 copy.130
  263.6 1.9 fusion.223
  265.5 58.0 %reduce-scatter.4.cloned.1.call-done = f32[64,384]{1,0:T(8,128)} async-done(((f32[512,384]{1,0:T(8,128)}), f32[64,384]{1,0:T(8,128)}) %reduce-scatter.4.cloned.1.call-update) | async-done | bytes 98320
  328.7 4.1 %all-to-all-start = ((f32[4,1,6144]{2,1,0:T(1,128)}), f32[4,1,6144]{2,1,0:T(1,128)}, u32[]{:S(2)}, u32[]{:S(2)}) async-start(f32[4,1,6144]{2,1,0:T(1,128)} %reshape.133), calls=%async_computation | async-start | bytes 196608 | tf_op jit(solution)/shard_map/all_to_all | solution.py:191
  332.8 3.0 broadcast_divide_fusion
  (561 shorter events, 210.0 us)
Async XLA Ops:
  7.2 316.3 %reduce-scatter.4.cloned.1.call-start = ((), (), s32[]{:S(2)}) async-start(), calls=%async_computation.2 | async-start | bytes 884736
  7.2 85.3 %copy-start.57 = (f32[64,768]{1,0:T(8,128)S(1)}, f32[64,768]{1,0:T(8,128)}, u32[]{:S(2)}) copy-start(f32[64,768]{1,0:T(8,128)} %param.11) | copy-start | bytes 589828
  94.0 20.7 %collective-permute-start.7 = (f32[3,64,12]{2,1,0:T(8,128)}, f32[3,64,12]{2,1,0:T(8,128)}, u32[]{:S(2)}, u32[]{:S(2)}) collective-permute-start(f32[3,64,12]{2,1,0:T(8,128)} %get-tuple-element.89), channel_id=1, source_target_pairs={{0,1},{1,2},{2,3},{3,0},{4,5},{5,6},{6,7},{7,4},{8,9},{9,10},{10,1... | collective-permute-start | bytes 27656 | tf_op jit(solution)/shard_map/ppermute | solution.py:22
  94.5 14.2 %collective-permute-start = (f32[1,768]{1,0:T(1,128)S(1)}, f32[1,768]{1,0:T(1,128)S(1)}, u32[]{:S(2)}, u32[]{:S(2)}) collective-permute-start(f32[1,768]{1,0:T(1,128)S(1)} %get-tuple-element.72), channel_id=1, source_target_pairs={{4,0},{8,4},{12,8},{16,12},{20,16},{24,20},{28,24},{0,28},{5,1},{9... | collective-permute-start | bytes 9224 | tf_op jit(solution)/shard_map/ppermute | solution.py:25
  100.1 8.7 %collective-permute-start.6 = (f32[64,12]{1,0:T(8,128)S(1)}, f32[64,12]{1,0:T(8,128)S(1)}, u32[]{:S(2)}, u32[]{:S(2)}) collective-permute-start(f32[64,12]{1,0:T(8,128)S(1)} %get-tuple-element.95), channel_id=1, source_target_pairs={{0,1},{1,2},{2,3},{3,0},{4,5},{5,6},{6,7},{7,4},{8,9},{9,10},{10,1... | collective-permute-start | bytes 9224 | tf_op jit(solution)/shard_map/ppermute | solution.py:22
  101.4 7.4 %collective-permute-start.2 = (f32[1,768]{1,0:T(1,128)S(1)}, f32[1,768]{1,0:T(1,128)S(1)}, u32[]{:S(2)}, u32[]{:S(2)}) collective-permute-start(f32[1,768]{1,0:T(1,128)S(1)} %get-tuple-element.73), channel_id=1, source_target_pairs={{0,4},{4,8},{8,12},{12,16},{16,20},{20,24},{24,28},{28,0},{1,5},{5... | collective-permute-start | bytes 9224 | tf_op jit(solution)/shard_map/ppermute | solution.py:22
  101.4 12.2 %collective-permute-start.4 = (f32[64,12]{1,0:T(8,128)S(1)}, f32[64,12]{1,0:T(8,128)}, u32[]{:S(2)}, u32[]{:S(2)}) collective-permute-start(f32[64,12]{1,0:T(8,128)S(1)} %get-tuple-element.94), channel_id=1, source_target_pairs={{1,0},{2,1},{3,2},{0,3},{5,4},{6,5},{7,6},{4,7},{9,8},{10,9},{11,1... | collective-permute-start | bytes 9224 | tf_op jit(solution)/shard_map/ppermute | solution.py:25
  108.6 6.1 %collective-permute-start.5 = (f32[3,64,12]{2,1,0:T(8,128)}, f32[3,64,12]{2,1,0:T(8,128)S(1)}, u32[]{:S(2)}, u32[]{:S(2)}) collective-permute-start(f32[3,64,12]{2,1,0:T(8,128)} %get-tuple-element.88), channel_id=1, source_target_pairs={{1,0},{2,1},{3,2},{0,3},{5,4},{6,5},{7,6},{4,7},{9,8},{10,9},{11,1... | collective-permute-start | bytes 27656 | tf_op jit(solution)/shard_map/ppermute | solution.py:25
  108.8 6.6 %collective-permute-start.3 = (f32[3,1,768]{2,1,0:T(1,128)}, f32[3,1,768]{2,1,0:T(1,128)S(1)}, u32[]{:S(2)}, u32[]{:S(2)}) collective-permute-start(f32[3,1,768]{2,1,0:T(1,128)} %get-tuple-element.87), channel_id=1, source_target_pairs={{0,4},{4,8},{8,12},{12,16},{16,20},{20,24},{24,28},{28,0},{1,5},{5... | collective-permute-start | bytes 27656 | tf_op jit(solution)/shard_map/ppermute | solution.py:22
  108.8 6.5 %collective-permute-start.1 = (f32[3,1,768]{2,1,0:T(1,128)S(1)}, f32[3,1,768]{2,1,0:T(1,128)S(1)}, u32[]{:S(2)}, u32[]{:S(2)}) collective-permute-start(f32[3,1,768]{2,1,0:T(1,128)S(1)} %get-tuple-element.86), channel_id=1, source_target_pairs={{4,0},{8,4},{12,8},{16,12},{20,16},{24,20},{28,24},{0,28},{5,1},{9... | collective-permute-start | bytes 27656 | tf_op jit(solution)/shard_map/ppermute | solution.py:25
  114.7 34.0 %copy-start.33 = (f32[64,768]{1,0:T(8,128)}, f32[64,768]{1,0:T(8,128)S(1)}, u32[]{:S(2)}) copy-start(f32[64,768]{1,0:T(8,128)S(1)} %get-tuple-element.90) | copy-start | bytes 589828
  121.2 27.5 %collective-permute-start.11 = (f32[3,64,12]{2,1,0:T(8,128)}, f32[3,64,12]{2,1,0:T(8,128)}, u32[]{:S(2)}, u32[]{:S(2)}) collective-permute-start(f32[3,64,12]{2,1,0:T(8,128)} %get-tuple-element.85), channel_id=1, source_target_pairs={{0,1},{1,2},{2,3},{3,0},{4,5},{5,6},{6,7},{7,4},{8,9},{9,10},{10,1... | collective-permute-start | bytes 27656 | tf_op jit(solution)/shard_map/ppermute | solution.py:22
  121.2 27.5 %collective-permute-start.10 = (f32[3,64,12]{2,1,0:T(8,128)}, f32[3,64,12]{2,1,0:T(8,128)}, u32[]{:S(2)}, u32[]{:S(2)}) collective-permute-start(f32[3,64,12]{2,1,0:T(8,128)} %get-tuple-element.84), channel_id=1, source_target_pairs={{1,0},{2,1},{3,2},{0,3},{5,4},{6,5},{7,6},{4,7},{9,8},{10,9},{11,1... | collective-permute-start | bytes 27656 | tf_op jit(solution)/shard_map/ppermute | solution.py:25
  122.9 25.7 %collective-permute-start.9 = (f32[3,1,768]{2,1,0:T(1,128)}, f32[3,1,768]{2,1,0:T(1,128)S(1)}, u32[]{:S(2)}, u32[]{:S(2)}) collective-permute-start(f32[3,1,768]{2,1,0:T(1,128)} %get-tuple-element.83), channel_id=1, source_target_pairs={{0,4},{4,8},{8,12},{12,16},{16,20},{20,24},{24,28},{28,0},{1,5},{5... | collective-permute-start | bytes 27656 | tf_op jit(solution)/shard_map/ppermute | solution.py:22
  122.9 25.7 %collective-permute-start.8 = (f32[3,1,768]{2,1,0:T(1,128)}, f32[3,1,768]{2,1,0:T(1,128)}, u32[]{:S(2)}, u32[]{:S(2)}) collective-permute-start(f32[3,1,768]{2,1,0:T(1,128)} %get-tuple-element.82), channel_id=1, source_target_pairs={{4,0},{8,4},{12,8},{16,12},{20,16},{24,20},{28,24},{0,28},{5,1},{9... | collective-permute-start | bytes 27656 | tf_op jit(solution)/shard_map/ppermute | solution.py:25
  156.3 27.4 %collective-permute-start.15 = (f32[3,64,12]{2,1,0:T(8,128)}, f32[3,64,12]{2,1,0:T(8,128)}, u32[]{:S(2)}, u32[]{:S(2)}) collective-permute-start(f32[3,64,12]{2,1,0:T(8,128)} %get-tuple-element.81), channel_id=1, source_target_pairs={{0,1},{1,2},{2,3},{3,0},{4,5},{5,6},{6,7},{7,4},{8,9},{9,10},{10,1... | collective-permute-start | bytes 27656 | tf_op jit(solution)/shard_map/ppermute | solution.py:22
  156.3 27.4 %collective-permute-start.14 = (f32[3,64,12]{2,1,0:T(8,128)}, f32[3,64,12]{2,1,0:T(8,128)}, u32[]{:S(2)}, u32[]{:S(2)}) collective-permute-start(f32[3,64,12]{2,1,0:T(8,128)} %get-tuple-element.80), channel_id=1, source_target_pairs={{1,0},{2,1},{3,2},{0,3},{5,4},{6,5},{7,6},{4,7},{9,8},{10,9},{11,1... | collective-permute-start | bytes 27656 | tf_op jit(solution)/shard_map/ppermute | solution.py:25
  158.0 25.7 %collective-permute-start.13 = (f32[3,1,768]{2,1,0:T(1,128)}, f32[3,1,768]{2,1,0:T(1,128)S(1)}, u32[]{:S(2)}, u32[]{:S(2)}) collective-permute-start(f32[3,1,768]{2,1,0:T(1,128)} %get-tuple-element.79), channel_id=1, source_target_pairs={{0,4},{4,8},{8,12},{12,16},{16,20},{20,24},{24,28},{28,0},{1,5},{5... | collective-permute-start | bytes 27656 | tf_op jit(solution)/shard_map/ppermute | solution.py:22
  158.0 25.7 %collective-permute-start.12 = (f32[3,1,768]{2,1,0:T(1,128)}, f32[3,1,768]{2,1,0:T(1,128)}, u32[]{:S(2)}, u32[]{:S(2)}) collective-permute-start(f32[3,1,768]{2,1,0:T(1,128)} %get-tuple-element.78), channel_id=1, source_target_pairs={{4,0},{8,4},{12,8},{16,12},{20,16},{24,20},{28,24},{0,28},{5,1},{9... | collective-permute-start | bytes 27656 | tf_op jit(solution)/shard_map/ppermute | solution.py:25
  192.3 28.2 %collective-permute-start.19 = (f32[3,64,12]{2,1,0:T(8,128)}, f32[3,64,12]{2,1,0:T(8,128)}, u32[]{:S(2)}, u32[]{:S(2)}) collective-permute-start(f32[3,64,12]{2,1,0:T(8,128)} %get-tuple-element.77), channel_id=1, source_target_pairs={{0,1},{1,2},{2,3},{3,0},{4,5},{5,6},{6,7},{7,4},{8,9},{9,10},{10,1... | collective-permute-start | bytes 27656 | tf_op jit(solution)/shard_map/ppermute | solution.py:22
  192.3 28.2 %collective-permute-start.18 = (f32[3,64,12]{2,1,0:T(8,128)}, f32[3,64,12]{2,1,0:T(8,128)}, u32[]{:S(2)}, u32[]{:S(2)}) collective-permute-start(f32[3,64,12]{2,1,0:T(8,128)} %get-tuple-element.76), channel_id=1, source_target_pairs={{1,0},{2,1},{3,2},{0,3},{5,4},{6,5},{7,6},{4,7},{9,8},{10,9},{11,1... | collective-permute-start | bytes 27656 | tf_op jit(solution)/shard_map/ppermute | solution.py:25
  194.0 26.4 %collective-permute-start.17 = (f32[3,1,768]{2,1,0:T(1,128)}, f32[3,1,768]{2,1,0:T(1,128)S(1)}, u32[]{:S(2)}, u32[]{:S(2)}) collective-permute-start(f32[3,1,768]{2,1,0:T(1,128)} %get-tuple-element.75), channel_id=1, source_target_pairs={{0,4},{4,8},{8,12},{12,16},{16,20},{20,24},{24,28},{28,0},{1,5},{5... | collective-permute-start | bytes 27656 | tf_op jit(solution)/shard_map/ppermute | solution.py:22
  194.0 26.4 %collective-permute-start.16 = (f32[3,1,768]{2,1,0:T(1,128)}, f32[3,1,768]{2,1,0:T(1,128)}, u32[]{:S(2)}, u32[]{:S(2)}) collective-permute-start(f32[3,1,768]{2,1,0:T(1,128)} %get-tuple-element.74), channel_id=1, source_target_pairs={{4,0},{8,4},{12,8},{16,12},{20,16},{24,20},{28,24},{0,28},{5,1},{9... | collective-permute-start | bytes 27656 | tf_op jit(solution)/shard_map/ppermute | solution.py:25
  328.7 8.3 %all-to-all-start = ((f32[4,1,6144]{2,1,0:T(1,128)}), f32[4,1,6144]{2,1,0:T(1,128)}, u32[]{:S(2)}, u32[]{:S(2)}) async-start(f32[4,1,6144]{2,1,0:T(1,128)} %reshape.133), calls=%async_computation | async-start | bytes 196608 | tf_op jit(solution)/shard_map/all_to_all | solution.py:191
  (62 other events, 145.1 us)
Sparse Core Ops, SparseCore 0:
  263.7 59.7 reduce-scatter.3
where the time goes:
time: 358 us; the launch traced here: 353 us
  local copies, waits for them, and re-layouts  167 us (47%)
  waiting for transfers between devices  59.8 us (17%)
  other arithmetic  42.9 us (12%)
  starting transfers between devices  36.3 us (10%)
  matrix products  29.2 us (8%)
  between operations  14.9 us (4%)
    unnamed x2, waiting for transfers between devices  58 us
    dynamic_slice x64, local copies, waits for them, and re-layouts, lookup(): values = lax.map(one_row, grains)  48.4 us
    ppermute x10, starting transfers between devices, padded(): lax.ppermute(lax.slice_in_dim(block, 0, width, axis=dim), axis, backward)  30.4 us
    another operation x24, local copies, waits for them, and re-layouts, cross(): jnp.stack([first[1] * second[2] - first[2] * second[1], first[2] * second...  29.4 us
    dot_general x64, matrix products, one_row(): return jnp.dot(table_rows, onehot, precision=lax.Precision.HIGHEST)  21.3 us
    sub x8, local copies, waits for them, and re-layouts, cross(): first[1] * second[2] - first[2] * second[1]  13 us
    sub x8, local copies, waits for them, and re-layouts, cross(): first[2] * second[0] - first[0] * second[2]  13 us
    sub x8, local copies, waits for them, and re-layouts, cross(): first[0] * second[1] - first[1] * second[0]  12.1 us
  transfers between devices with their start and end apart: 22, of which 3 were waited for; matrix products, arithmetic and copies ran while one was open for 22% of the time, Pallas kernels for 0%

commit v1 on v0

v1 whole, which is shorter than its diff:
```python
import functools
import math

import jax
import jax.numpy as jnp
import numpy as np
from jax import lax
from jax.experimental import pallas as pl
from jax.experimental.pallas import tpu as pltpu
from jax.sharding import PartitionSpec as P
import ml_dtypes

NZ = 12
STEPS = 4
DAMPING = 0.5
TIME_STEP = 0.12
LANES = 128
SUB = 8
MESH = pl.DeviceIdType.MESH


def iota(shape, dim):
    return lax.broadcasted_iota(jnp.int32, shape, dim)


def sin_cos(x):
    turns = jnp.floor(x * (2.0 / math.pi) + 0.5)
    quadrant = turns.astype(jnp.int32)
    r = x - turns * 1.5703125
    r = r - turns * 4.837512969970703125e-4
    r = r - turns * 7.549789948768648e-8
    z = r * r
    sine = r + r * z * (-1.6666654611e-1 + z * (8.3321608736e-3 - z * 1.9515295891e-4))
    cosine = 1.0 - 0.5 * z + z * z * (
        4.166664568298827e-2 + z * (-1.388731625493765e-3 + z * 2.443315711809948e-5)
    )
    odd = (quadrant & 1) == 1
    s = jnp.where(odd, cosine, sine)
    c = jnp.where(odd, sine, cosine)
    s = jnp.where((quadrant & 2) == 2, -s, s)
    c = jnp.where(((quadrant + 1) & 2) == 2, -c, c)
    return s, c


def neighbours(ngx, ngy):
    gx, gy = lax.axis_index("gx"), lax.axis_index("gy")
    return (
        gx,
        gy,
        lax.rem(gx + 1, ngx),
        lax.rem(gx + ngx - 1, ngx),
        lax.rem(gy + 1, ngy),
        lax.rem(gy + ngy - 1, ngy),
    )


def halo_kernel(
    ngx, ngy, p_ref, a_ref, g_ref, rows_out, cols_out, corners_out,
    rows_msg, cols_msg, corners_msg, send, recv,
):
    gx, gy, down, up, right, left = neighbours(ngx, ngy)
    around = [
        (up, gy), (down, gy), (gx, left), (gx, right),
        (up, left), (up, right), (down, left), (down, right),
    ]
    barrier = pltpu.get_barrier_semaphore()
    for device in around:
        pl.semaphore_signal(barrier, inc=1, device_id=device, device_id_type=MESH)

    rows, columns = p_ref.shape
    half = columns // 2
    near = (slice(0, SUB), slice(rows - SUB, rows))
    side = (slice(0, LANES), slice(columns - LANES, columns))
    sub_low = iota((SUB, columns), 0) < 4
    for k in range(2):
        own = sub_low if k == 0 else jnp.logical_not(sub_low)
        g = g_ref[near[k], :].astype(jnp.float32)
        rows_msg[k, :, :columns] = jnp.where(
            own, p_ref[near[k], :], pltpu.roll(a_ref[near[k], :], 4, 0)
        )
        rows_msg[k, :, columns:] = jnp.where(
            own[:, :half], g[:, :half], pltpu.roll(g[:, half:], 4, 0)
        )
    lane_low = iota((rows, LANES), 1) < 64
    for k in range(2):
        own = lane_low if k == 0 else jnp.logical_not(lane_low)
        g = g_ref[:, side[k]].astype(jnp.float32)
        cols_msg[k, :rows] = jnp.where(own, p_ref[:, side[k]], pltpu.roll(a_ref[:, side[k]], 64, 1))
        cols_msg[k, rows:] = jnp.where(
            own[: rows // 2], g[: rows // 2], pltpu.roll(g[rows // 2 :], 64, 1)
        )
    tile_sub = iota((SUB, LANES), 0) < 4
    tile_lane = iota((SUB, LANES), 1) < 64
    for k in range(2):
        for j in range(2):
            own_sub = tile_sub if k == 0 else jnp.logical_not(tile_sub)
            own_lane = tile_lane if j == 0 else jnp.logical_not(tile_lane)
            g = g_ref[near[k], side[j]].astype(jnp.float32)
            corners_msg[2 * k + j] = jnp.where(
                own_sub,
                jnp.where(own_lane, p_ref[near[k], side[j]], pltpu.roll(a_ref[near[k], side[j]], 64, 1)),
                pltpu.roll(g, 4, 0),
            )
    pl.semaphore_wait(barrier, 8)
    sources = [rows_msg.at[0], rows_msg.at[1], cols_msg.at[0], cols_msg.at[1]]
    sources += [corners_msg.at[k] for k in range(4)]
    targets = [rows_out.at[0], rows_out.at[1], cols_out.at[0], cols_out.at[1]]
    targets += [corners_out.at[k] for k in range(4)]
    copies = [
        pltpu.make_async_remote_copy(
            src_ref=sources[k], dst_ref=targets[k], send_sem=send.at[k], recv_sem=recv.at[k],
            device_id=around[k], device_id_type=MESH,
        )
        for k in range(8)
    ]
    for copy in copies:
        copy.start()
    for copy in copies:
        copy.wait()


def halo(ngx, ngy, polar, azimuth, grains):
    rows, columns = polar.shape
    shapes = [(2, SUB, columns + columns // 2), (2, rows + rows // 2, LANES), (4, SUB, LANES)]
    vmem = pl.BlockSpec(memory_space=pltpu.VMEM)
    return pl.pallas_call(
        functools.partial(halo_kernel, ngx, ngy),
        out_shape=[jax.ShapeDtypeStruct(s, jnp.float32) for s in shapes],
        in_specs=[vmem] * 3,
        out_specs=[vmem] * 3,
        scratch_shapes=[pltpu.VMEM(s, jnp.float32) for s in shapes]
        + [pltpu.SemaphoreType.DMA((8,)), pltpu.SemaphoreType.DMA((8,))],
        compiler_params=pltpu.CompilerParams(
            collective_id=0, has_side_effects=True, vmem_limit_bytes=16 * 2**20
        ),
        name="halo",
    )(polar, azimuth, grains)


def steps_kernel(
    ngx, p_ref, a_ref, g_ref, rows_ref, cols_ref, corners_ref,
    stiff_ref, anis_ref, apol_ref, aazi_ref, applied_ref,
    moment_ref, layer_ref, m_ref, w_ref, coef_ref, axis_ref,
):
    rows, columns = p_ref.shape
    strips, tiles = rows // SUB, columns // LANES
    half = columns // 2
    lane = iota((SUB, LANES), 1)
    sub = iota((SUB, LANES), 0)
    sub_low, lane_low = sub < 4, lane < 64

    def raw(s, t):
        if s < strips and t < tiles:
            r, c = slice(s * SUB, s * SUB + SUB), slice(t * LANES, t * LANES + LANES)
            return p_ref[r, c], a_ref[r, c], g_ref[r, c]
        if s < strips:
            r = slice(s * SUB, s * SUB + SUB)
            k = (s * SUB) % (rows // 2) + rows
            rg = slice(k, k + SUB)
            fr, fl = cols_ref[0, r, :], cols_ref[1, r, :]
            gr, gl = cols_ref[0, rg, :], cols_ref[1, rg, :]
            p = jnp.where(lane_low, fr, fl)
            a = pltpu.roll(jnp.where(lane_low, fl, fr), 64, 1)
            if s * SUB < rows // 2:
                g = jnp.where(lane_low, gr, gl)
            else:
                g = pltpu.roll(jnp.where(lane_low, gl, gr), 64, 1)
        elif t < tiles:
            c = slice(t * LANES, t * LANES + LANES)
            k = (t * LANES) % half + columns
            cg = slice(k, k + LANES)
            fn, fp = rows_ref[0, :, c], rows_ref[1, :, c]
            gn, gp = rows_ref[0, :, cg], rows_ref[1, :, cg]
            p = jnp.where(sub_low, fn, fp)
            a = pltpu.roll(jnp.where(sub_low, fp, fn), 4, 0)
            if t * LANES < half:
                g = jnp.where(sub_low, gn, gp)
            else:
                g = pltpu.roll(jnp.where(sub_low, gp, gn), 4, 0)
        else:
            q = [corners_ref[k] for k in range(4)]
            p = jnp.where(sub_low, jnp.where(lane_low, q[0], q[1]), jnp.where(lane_low, q[2], q[3]))
            a = jnp.where(sub_low, jnp.where(lane_low, q[1], q[0]), jnp.where(lane_low, q[3], q[2]))
            a = pltpu.roll(a, 64, 1)
            g = jnp.where(sub_low, jnp.where(lane_low, q[2], q[3]), jnp.where(lane_low, q[0], q[1]))
            g = pltpu.roll(g, 4, 0)
        return p, a, g.astype(jnp.int32)

    def store(ref, lead, s, t, value):
        ref[(*lead, t, slice(SUB + s * SUB, 2 * SUB + s * SUB), slice(None))] = value
        if s == 0:
            k = SUB * (strips + 2)
            ref[(*lead, t, slice(k, k + SUB), slice(None))] = value
        if s == strips:
            ref[(*lead, t, slice(0, SUB), slice(None))] = value

    def rows_of(ref, lead, s, t, shift=0):
        k = SUB + s * SUB + shift
        return ref[(*lead, t, slice(k, k + SUB), slice(None))]

    sp, cp = sin_cos(apol_ref[...])
    sa, ca = sin_cos(aazi_ref[...])
    root = jnp.sqrt(anis_ref[...])
    tables = [stiff_ref[...], root * sp * ca, root * sp * sa, root * cp]
    pages = [
        [jnp.broadcast_to(table[:, k : k + LANES], (SUB, LANES)) for k in range(0, table.shape[1], LANES)]
        for table in tables
    ]

    for s in range(strips + 1):
        for t in range(tiles + 1):
            p, a, g = raw(s, t)
            sp, cp = sin_cos(p)
            sa, ca = sin_cos(a)
            for c, value in enumerate((sp * ca, sp * sa, cp)):
                store(m_ref, (0, c), s, t, value)
            place = g & (LANES - 1)
            page = g >> 7
            found = []
            for table in pages:
                value = jnp.take_along_axis(table[0], place, axis=1, mode="promise_in_bounds")
                for k in range(1, len(table)):
                    other = jnp.take_along_axis(table[k], place, axis=1, mode="promise_in_bounds")
                    value = jnp.where(page == k, other, value)
                found.append(value)
            store(w_ref, (), s, t, found[0])
            for c in range(3):
                axis_ref[c, t, s * SUB : s * SUB + SUB, :] = found[1 + c]

    count = tiles + 1

    def shifter(values, shift):
        turned = {}

        def turn(t):
            t = t % count
            if t not in turned:
                turned[t] = pltpu.roll(values[t], (-shift) % LANES, 1)
            return turned[t]

        def at(t):
            if shift > 0:
                return jnp.where(lane < LANES - shift, turn(t), turn(t + 1))
            return jnp.where(lane >= -shift, turn(t), turn(t - 1))

        return at

    def couple(p, q):
        return 2.0 * p * q / (p + q)

    for s in range(strips + 1):
        here = [rows_of(w_ref, (), s, t) for t in range(count)]
        plus_y = shifter(here, NZ)
        plus_z = shifter(here, 1)
        y_link = [couple(here[t], plus_y(t)) for t in range(count)]
        z_link = []
        for t in range(count):
            spot = t * LANES + lane
            if t == tiles:
                spot = jnp.where(lane_low, spot, spot - count * LANES + NZ * LANES)
            level = spot - NZ * ((spot * 43691) >> 19)
            z_link.append(jnp.where(level < NZ - 1, couple(here[t], plus_z(t)), 0.0))
        y_back = shifter(y_link, -NZ)
        z_back = shifter(z_link, -1)
        for t in range(count):
            links = [
                couple(here[t], rows_of(w_ref, (), s, t, 1)),
                couple(here[t], rows_of(w_ref, (), s, t, -1)),
                y_link[t],
                y_back(t),
                z_link[t],
                z_back(t),
            ]
            total = links[0] + links[1] + links[2] + links[3] + links[4] + links[5]
            for k, value in enumerate(links + [total]):
                coef_ref[k, t, s * SUB : s * SUB + SUB, :] = value

    applied = [applied_ref[c] for c in range(3)]
    factor = TIME_STEP / (1.0 + DAMPING * DAMPING)

    def one_step(index, carry):
        now = lax.rem(index, 2)
        later = 1 - now
        for s in range(strips + 1):
            here = [[rows_of(m_ref, (now, c), s, t) for t in range(count)] for c in range(3)]
            shifts = [[shifter(here[c], k) for k in (NZ, -NZ, 1, -1)] for c in range(3)]
            for t in range(count):
                spot = (t, slice(s * SUB, s * SUB + SUB), slice(None))
                link = [coef_ref[(k, *spot)] for k in range(7)]
                easy = [axis_ref[(c, *spot)] for c in range(3)]
                m = [here[c][t] for c in range(3)]
                project = easy[0] * m[0] + easy[1] * m[1] + easy[2] * m[2]
                h = []
                for c in range(3):
                    value = link[0] * rows_of(m_ref, (now, c), s, t, 1)
                    value = value + link[1] * rows_of(m_ref, (now, c), s, t, -1)
                    for k in range(4):
                        value = value + link[2 + k] * shifts[c][k](t)
                    value = value - link[6] * m[c]
                    h.append(value + project * easy[c] + applied[c])

                def cross(f, g):
                    return [
                        f[1] * g[2] - f[2] * g[1],
                        f[2] * g[0] - f[0] * g[2],
                        f[0] * g[1] - f[1] * g[0],
                    ]

                torque = cross(m, h)
                damped = cross(m, torque)
                moved = [
                    m[c] - (factor * torque[c] + (factor * DAMPING) * damped[c]) for c in range(3)
                ]
                size = moved[0] * moved[0] + moved[1] * moved[1] + moved[2] * moved[2]
                inverse = lax.rsqrt(size)
                for c in range(3):
                    store(m_ref, (later, c), s, t, moved[c] * inverse)
        return carry

    lax.fori_loop(0, STEPS, one_step, 0)

    last = STEPS % 2
    width_y = columns // NZ
    per = width_y // ngx
    row = iota((ngx * SUB, columns), 0)
    column = iota((ngx * SUB, columns), 1)
    cell = (row // SUB) * per + row % SUB
    inside = (column >= cell * NZ) & (column < cell * NZ + NZ) & (row % SUB < per)
    chooser = jnp.where(inside, 1.0, 0.0).astype(jnp.bfloat16)
    for c in range(3):
        for t in range(tiles):
            moment_ref[c, :, t * LANES : t * LANES + LANES] = m_ref[last, c, t, SUB : SUB + rows, :]
        whole = moment_ref[c]
        high = whole.astype(jnp.bfloat16)
        low = (whole - high.astype(jnp.float32)).astype(jnp.bfloat16)
        sums = sum(
            lax.dot_general(
                chooser, part, (((1,), (1,)), ((), ())), preferred_element_type=jnp.float32
            )
            for part in (low, high)
        )
        layer_ref[:, c * rows : c * rows + rows] = sums * (1.0 / math.sqrt(NZ))
    layer_ref[:, 3 * rows :] = jnp.zeros((ngx * SUB, rows), jnp.float32)


def steps(ngx, polar, azimuth, grains, ghosts, tables, applied):
    rows, columns = polar.shape
    vmem = pl.BlockSpec(memory_space=pltpu.VMEM)
    strips, tiles = rows // SUB + 1, columns // LANES + 1
    return pl.pallas_call(
        functools.partial(steps_kernel, ngx),
        out_shape=[
            jax.ShapeDtypeStruct((3, rows, columns), jnp.float32),
            jax.ShapeDtypeStruct((ngx * SUB, 4 * rows), jnp.float32),
        ],
        in_specs=[vmem] * 10 + [pl.BlockSpec(memory_space=pltpu.SMEM)],
        out_specs=[vmem] * 2,
        scratch_shapes=[
            pltpu.VMEM((2, 3, tiles, SUB * (strips + 2), LANES), jnp.float32),
            pltpu.VMEM((tiles, SUB * (strips + 2), LANES), jnp.float32),
            pltpu.VMEM((7, tiles, SUB * strips, LANES), jnp.float32),
            pltpu.VMEM((3, tiles, SUB * strips, LANES), jnp.float32),
        ],
        compiler_params=pltpu.CompilerParams(vmem_limit_bytes=32 * 2**20),
        name="steps",
    )(polar, azimuth, grains, *ghosts, *tables, applied)


def split(values):
    high = values.astype(ml_dtypes.bfloat16)
    low = (values - high.astype(np.float64)).astype(ml_dtypes.bfloat16)
    return high, low


def wave_tables(ngx, ngy, width_x, width_y):
    total_x, total_y = width_x * ngx, width_y * ngy
    devices = ngx * ngy
    per_x, per_y = width_x // ngy, width_y // ngx
    x = np.arange(total_x)
    angle = 2.0 * np.pi / total_x * (np.outer(x, x) % total_x)
    both = np.stack([np.cos(angle), -np.sin(angle)], axis=1).reshape(total_x, 2, devices, per_x)
    table_x = both.transpose(0, 2, 1, 3).reshape(total_x, 2 * total_x)
    y = np.arange(total_y)
    angle = 2.0 * np.pi / total_y * (np.outer(y, y) % total_y)
    both = np.concatenate([np.cos(angle), np.sin(angle)], axis=1)
    table_y = np.zeros((devices, SUB, 2 * total_y))
    table_y[:, :per_y] = both.reshape(devices, per_y, 2 * total_y)
    return (*split(table_x), *split(table_y.reshape(devices * SUB, 2 * total_y)))


def two_parts(value):
    high = value.astype(jnp.bfloat16).astype(jnp.float32)
    return jnp.concatenate([high, value - high], axis=0).astype(jnp.bfloat16)


def product(value, high_ref, low_ref):
    rows = value.shape[0]
    parts = two_parts(value)
    big = jnp.dot(parts, high_ref[...], preferred_element_type=jnp.float32)
    head = -(-rows // 16) * 16
    small = jnp.dot(parts[:head], low_ref[...], preferred_element_type=jnp.float32)
    return (big[rows:] + small[:rows]) + big[:rows]


def waves_kernel(
    ngx, ngy, layer_ref, xh_hbm, xl_hbm, yh_hbm, yl_hbm, flip_ref, non_ref,
    xh, xl, yh, yl, lines, message, held, load, send_x, recv_x, send_y, recv_y,
):
    gx, gy = lax.axis_index("gx"), lax.axis_index("gy")
    devices = ngx * ngy
    me = gx * ngy + gy
    width_x = layer_ref.shape[1] // 4
    total_x = ngx * width_x
    per_x = width_x // ngy
    total_y = yh.shape[1] // 2
    loads = [
        pltpu.make_async_copy(source, target, load.at[k])
        for k, (source, target) in enumerate([(xh_hbm, xh), (xl_hbm, xl), (yh_hbm, yh), (yl_hbm, yl)])
    ]
    barrier = pltpu.get_barrier_semaphore()

    def greet(k, carry):
        other = lax.rem(me + k, devices)
        pl.semaphore_signal(
            barrier, inc=1, device_id=(other // ngy, other % ngy), device_id_type=MESH
        )
        return carry

    lax.fori_loop(1, devices, greet, 0)
    for copy in loads:
        copy.start()
    pl.semaphore_wait(barrier, devices - 1)

    def line_copy(k):
        other = lax.rem(gx + k, ngx)
        source = lax.rem(gx + ngx - k, ngx)
        return pltpu.make_async_remote_copy(
            src_ref=layer_ref.at[pl.ds(pl.multiple_of(other * SUB, SUB), SUB)],
            dst_ref=lines.at[gx], send_sem=send_x.at[k], recv_sem=recv_x.at[k],
            device_id=(other, gy), device_id_type=MESH,
        )

    for k in range(1, ngx):
        line_copy(k).start()
    lines[gx] = layer_ref[pl.ds(pl.multiple_of(gx * SUB, SUB), SUB), :]
    for k in range(1, ngx):
        line_copy(k).wait()
    loads[0].wait()
    loads[1].wait()

    whole = jnp.concatenate(
        [
            jnp.concatenate(
                [lines[s, :, c * width_x : c * width_x + width_x] for s in range(ngx)], axis=1
            )
            for c in range(3)
        ],
        axis=0,
    )
    waves = product(whole, xh, xl)
    wide = 2 * per_x
    blank = jnp.zeros((SUB, LANES - 3 * wide), jnp.float32)
    for d in range(devices):
        pieces = [waves[c * SUB : c * SUB + SUB, d * wide : d * wide + wide] for c in range(3)]
        message[d] = jnp.concatenate(pieces + [blank], axis=1)

    slot = gy * ngx + gx

    def wave_copy(k):
        other = lax.rem(me + k, devices)
        return pltpu.make_async_remote_copy(
            src_ref=message.at[other], dst_ref=held.at[slot],
            send_sem=send_y.at[k], recv_sem=recv_y.at[k],
            device_id=(other // ngy, other % ngy), device_id_type=MESH,
        )

    def start(k, carry):
        wave_copy(k).start()
        return carry

    def finish(k, carry):
        wave_copy(k).wait()
        return carry

    lax.fori_loop(1, devices, start, 0)
    held[slot] = message[me]
    loads[2].wait()
    loads[3].wait()
    lax.fori_loop(1, devices, finish, 0)

    table = held[...].reshape(devices * SUB, LANES).T
    spectrum = product(table, yh, yl) * (1.0 / math.sqrt(total_x * total_y))

    counter_x = me * per_x + iota((per_x, total_y), 0)
    counter_y = iota((per_x, total_y), 1)
    wave_x = jnp.where(counter_x < total_x // 2, counter_x, counter_x - total_x).astype(jnp.float32)
    wave_y = jnp.where(counter_y < total_y // 2, counter_y, counter_y - total_y).astype(jnp.float32)
    squared = wave_x * wave_x + wave_y * wave_y
    inverse = 1.0 / jnp.sqrt(jnp.maximum(squared, 1.0))
    beam_stop = jnp.where(squared > 0.5, 1.0, 0.0)
    unit_x, unit_y = wave_x * inverse, wave_y * inverse
    real, imag = [], []
    for c in range(3):
        re = spectrum[c * wide : c * wide + per_x]
        im = spectrum[c * wide + per_x : c * wide + wide]
        real.append(re[:, :total_y] + im[:, total_y:])
        imag.append(im[:, :total_y] - re[:, total_y:])
    flip = jnp.zeros_like(squared)
    non = jnp.zeros_like(squared)
    for part in (real, imag):
        along = unit_x * part[0] + unit_y * part[1]
        first = part[0] - unit_x * along
        second = part[1] - unit_y * along
        non = non + first * first
        flip = flip + second * second + part[2] * part[2]
    flip_ref[...] = flip * beam_stop
    non_ref[...] = non * beam_stop


def waves(ngx, ngy, width_x, width_y, layer):
    tables = wave_tables(ngx, ngy, width_x, width_y)
    devices = ngx * ngy
    vmem = pl.BlockSpec(memory_space=pltpu.VMEM)
    out = jax.ShapeDtypeStruct((width_x // ngy, width_y * ngy), jnp.float32)
    return pl.pallas_call(
        functools.partial(waves_kernel, ngx, ngy),
        out_shape=[out, out],
        in_specs=[vmem] + [pl.BlockSpec(memory_space=pl.ANY)] * 4,
        out_specs=[vmem] * 2,
        scratch_shapes=[pltpu.VMEM(t.shape, jnp.bfloat16) for t in tables]
        + [
            pltpu.VMEM((ngx, SUB, 4 * width_x), jnp.float32),
            pltpu.VMEM((devices, SUB, LANES), jnp.float32),
            pltpu.VMEM((devices, SUB, LANES), jnp.float32),
            pltpu.SemaphoreType.DMA((4,)),
            pltpu.SemaphoreType.DMA((ngx,)),
            pltpu.SemaphoreType.DMA((ngx,)),
            pltpu.SemaphoreType.DMA((devices,)),
            pltpu.SemaphoreType.DMA((devices,)),
        ],
        compiler_params=pltpu.CompilerParams(
            collective_id=1, has_side_effects=True, vmem_limit_bytes=56 * 2**20
        ),
        name="waves",
    )(layer, *[jnp.asarray(t) for t in tables])


def solution(mesh):
    ngx, ngy = mesh.shape["gx"], mesh.shape["gy"]

    def shards(polar, azimuth, grains, stiffness, anisotropy, axis_polar, axis_azimuth, applied):
        width_x, width_y = polar.shape[0], polar.shape[1] // NZ
        ghosts = halo(ngx, ngy, polar, azimuth, grains)
        tables = [t.reshape(1, -1) for t in (stiffness, anisotropy, axis_polar, axis_azimuth)]
        moment, layer = steps(ngx, polar, azimuth, grains, ghosts, tables, applied)
        flip, non = waves(ngx, ngy, width_x, width_y, layer)
        return (moment, flip, non)

    in_specs = (P("gx", "gy"), P("gx", "gy"), P("gx", "gy"), P(), P(), P(), P(), P())
    out_specs = (P(None, "gx", "gy"), P(("gx", "gy"), None), P(("gx", "gy"), None))
    return jax.shard_map(shards, mesh=mesh, in_specs=in_specs, out_specs=out_specs, check_vma=False)
```

time: 358 us -> 41.4 us (0.12); the launches traced: 353 us -> 41.1 us
  local copies, waits for them, and re-layouts: 167 us -> 5.96 us
  waiting for transfers between devices: 59.8 us -> 0 us
  other arithmetic: 42.9 us -> 0 us
  starting transfers between devices: 36.3 us -> 0 us
  Pallas kernels: 0 us -> 34.3 us
  matrix products: 29.2 us -> 0 us
  between operations: 14.9 us -> 0.75 us
    unnamed x2 -> x0, waiting for transfers between devices: 58 us -> none
    dynamic_slice x64 -> x0, local copies, waits for them, and re-layouts: 48.4 us -> none  [lookup(): values = lax.map(one_row, grains)]
    sub x24 -> x0, local copies, waits for them, and re-layouts: 38.1 us -> none  [the longest x8 13 us: cross(): first[1] * second[2] - first[2] * second[1]]
    pallas_call x0 -> x3, Pallas kernels: none -> 34.3 us  [the longest x1 16.9 us: waves(): pl.pallas_call(functools.partial(waves_kernel, ngx, ngy), out_shape=[out,...]
    another operation x28 -> x0, local copies, waits for them, and re-layouts: 33.6 us -> none  [the longest x24 29.4 us: cross(): jnp.stack([first[1] * second[2] - first[2] * second[1], first[2] * second...]
    ppermute x20 -> x0, starting transfers between devices: 32.1 us -> none  [the longest x10 30.4 us: padded(): lax.ppermute(lax.slice_in_dim(block, 0, width, axis=dim), axis, backward)]
    dot_general x70 -> x0, matrix products: 29.2 us -> none  [the longest x64 21.3 us: one_row(): return jnp.dot(table_rows, onehot, precision=lax.Precision.HIGHEST)]
    dynamic_update_slice x128 -> x0, local copies, waits for them, and re-layouts: 9.53 us -> none  [lookup(): values = lax.map(one_row, grains)]
  transfers between devices with their start and end apart: 22 -> 0, of which waited for: 3 -> 0; matrix products, arithmetic and copies ran while one was open for 22% -> 0% of each run, Pallas kernels for 0% -> 0%
where the time goes in v1:
time: 41.4 us; the launch traced here: 41.1 us
  Pallas kernels  34.3 us (83%)
  local copies, waits for them, and re-layouts  5.96 us (14%)
  between operations  0.75 us (2%)
    pallas_call x1, Pallas kernels, waves(): pl.pallas_call(functools.partial(waves_kernel, ngx, ngy), out_shape=[out,...  16.9 us
    pallas_call x1, Pallas kernels, halo(): pl.pallas_call(functools.partial(halo_kernel, ngx, ngy), out_shape=[jax.S...  9.51 us
    pallas_call x1, Pallas kernels, steps(): pl.pallas_call(functools.partial(steps_kernel, ngx), out_shape=[jax.Shape...  7.92 us
    unnamed x28, local copies, waits for them, and re-layouts  5.96 us

profile of v1, /device:TPU:0, one launch (start us, length us, event | category | flops | bytes accessed | tf_op | source)
XLA Modules:
  0.0 41.1 jit_solution(11155671361256230442)
XLA Ops:
  0.6 0.0 copy-start
  0.6 0.9 %copy-done = f32[64,768]{1,0:T(8,128)S(1)} copy-done((f32[64,768]{1,0:T(8,128)S(1)}, f32[64,768]{1,0:T(8,128)}, u32[]{:S(2)}) %copy-start) | copy-done | bytes 196632
  1.6 0.9 %copy-done.2 = f32[64,768]{1,0:T(8,128)S(1)} copy-done((f32[64,768]{1,0:T(8,128)S(1)}, f32[64,768]{1,0:T(8,128)}, u32[]{:S(2)}) %copy-start.2) | copy-done | bytes 196632
  2.5 0.9 %copy-done.4 = s32[64,768]{1,0:T(8,128)S(1)} copy-done((s32[64,768]{1,0:T(8,128)S(1)}, s32[64,768]{1,0:T(8,128)}, u32[]{:S(2)}) %copy-start.4) | copy-done | bytes 196632
  3.4 0.0 copy-start.9
  3.4 0.0 copy-start.10
  3.4 9.5 %halo.1 = (f32[2,8,1152]{2,1,0:T(8,128)S(1)}, f32[2,96,128]{2,1,0:T(8,128)S(1)}, f32[4,8,128]{2,1,0:T(8,128)S(1)}) custom-call(f32[64,768]{1,0:T(8,128)S(1)} %copy-done, f32[64,768]{1,0:T(8,128)S(1)} %copy-done.2, s32[64,768]{1,0:T(8,128)S(1)} %copy-done.4), custom_call_target="tpu_custom_call" | custom-call | tf_op jit(solution)/shard_map/halo/pallas_call | solution.py:126
  13.0 0.0 copy-start.7
  13.0 0.0 copy-start.11
  13.0 0.0 copy-done.1
  13.0 0.0 copy-done.3
  13.0 0.0 copy-done.5
  13.0 0.0 copy-done.8
  13.0 0.0 copy-done.9
  13.0 0.0 copy-done.10
  13.1 0.6 %copy-done.7 = f32[256]{0:T(256)S(1)} copy-done((f32[256]{0:T(256)S(1)}, f32[256]{0:T(256)}, u32[]{:S(2)}) %copy-start.7) | copy-done | bytes 1048
  13.7 0.0 copy-done.11
  13.7 7.9 %steps.1 = (f32[3,64,768]{2,1,0:T(8,128)}, f32[64,256]{1,0:T(8,128)S(1)}) custom-call(f32[64,768]{1,0:T(8,128)S(1)} %copy-done.1, f32[64,768]{1,0:T(8,128)S(1)} %copy-done.3, s32[64,768]{1,0:T(8,128)S(1)} %copy-done.5, f32[2,8,1152]{2,1,0:T(8,128)S(1)} %get-tuple-element.10.rows_ref, f32[2,96,128]{2,1,0:T(8,128)S(1)} %get-tuple-element.11.cols_ref, ...), custom_call_target="tpu_custom_call" | custom-call | tf_op jit(solution)/shard_map/steps/pallas_call | solution.py:350
  21.6 0.6 %copy-done.6 = f32[64,256]{1,0:T(8,128)} copy-done((f32[64,256]{1,0:T(8,128)}, f32[64,256]{1,0:T(8,128)S(1)}, u32[]{:S(2)}) %copy-start.6) | copy-done | bytes 65560
  22.2 16.9 %waves.1 = (f32[16,256]{1,0:T(8,128)}, f32[16,256]{1,0:T(8,128)}) custom-call(f32[64,256]{1,0:T(8,128)} %copy-done.6, bf16[512,1024]{1,0:T(8,128)(2,1)} %constant.8.clone.xh_hbm, bf16[512,1024]{1,0:T(8,128)(2,1)} %constant.9.clone.xl_hbm, bf16[256,512]{1,0:T(8,128)(2,1)} %constant.10.clone.yh_hbm, bf16[256,512]{1,0:T(8,128)(2,1)} %constant.11.clone.yl_hbm), custom_call_target="tpu_custom_call" | custom-call | tf_op jit(solution)/shard_map/waves/pallas_call | solution.py:525
  39.1 0.0 copy-start.12
  39.1 1.3 %copy.17 = f32[16,256]{1,0:T(8,128)} copy(f32[16,256]{1,0:T(8,128)} %get-tuple-element.21) | data formatting | bytes 32768
  40.5 0.0 copy-done.12
  40.5 0.6 %copy.18 = f32[16,256]{1,0:T(8,128)} copy(f32[16,256]{1,0:T(8,128)S(1)} %copy-done.12) | data formatting | bytes 32768
  (7 shorter events, 0.0 us)
Async XLA Ops:
  0.6 0.9 %copy-start = (f32[64,768]{1,0:T(8,128)S(1)}, f32[64,768]{1,0:T(8,128)}, u32[]{:S(2)}) copy-start(f32[64,768]{1,0:T(8,128)} %p_ref.3) | copy-start | bytes 589828
  1.6 0.9 %copy-start.2 = (f32[64,768]{1,0:T(8,128)S(1)}, f32[64,768]{1,0:T(8,128)}, u32[]{:S(2)}) copy-start(f32[64,768]{1,0:T(8,128)} %a_ref.3) | copy-start | bytes 589828
  2.5 0.9 %copy-start.4 = (s32[64,768]{1,0:T(8,128)S(1)}, s32[64,768]{1,0:T(8,128)}, u32[]{:S(2)}) copy-start(s32[64,768]{1,0:T(8,128)} %g_ref.3) | copy-start | bytes 589828
  3.4 9.6 %copy-start.1 = (f32[64,768]{1,0:T(8,128)S(1)}, f32[64,768]{1,0:T(8,128)}, u32[]{:S(2)}) copy-start(f32[64,768]{1,0:T(8,128)} %p_ref.3) | copy-start | bytes 589828
  3.4 9.6 %copy-start.3 = (f32[64,768]{1,0:T(8,128)S(1)}, f32[64,768]{1,0:T(8,128)}, u32[]{:S(2)}) copy-start(f32[64,768]{1,0:T(8,128)} %a_ref.3) | copy-start | bytes 589828
  3.4 9.6 %copy-start.5 = (s32[64,768]{1,0:T(8,128)S(1)}, s32[64,768]{1,0:T(8,128)}, u32[]{:S(2)}) copy-start(s32[64,768]{1,0:T(8,128)} %g_ref.3) | copy-start | bytes 589828
  3.4 9.6 %copy-start.8 = (f32[256]{0:T(256)S(1)}, f32[256]{0:T(256)}, u32[]{:S(2)}) copy-start(f32[256]{0:T(256)} %param.16) | copy-start | bytes 3076
  3.4 9.6 %copy-start.9 = (f32[256]{0:T(256)S(1)}, f32[256]{0:T(256)}, u32[]{:S(2)}) copy-start(f32[256]{0:T(256)} %param.17) | copy-start | bytes 3076
  3.4 9.6 %copy-start.10 = (f32[256]{0:T(256)S(1)}, f32[256]{0:T(256)}, u32[]{:S(2)}) copy-start(f32[256]{0:T(256)} %param.18) | copy-start | bytes 3076
  13.0 0.7 %copy-start.7 = (f32[256]{0:T(256)S(1)}, f32[256]{0:T(256)}, u32[]{:S(2)}) copy-start(f32[256]{0:T(256)} %param.15) | copy-start | bytes 3076
  13.0 0.7 %copy-start.11 = (f32[3]{0:T(128)S(1)}, f32[3]{0:T(128)}, u32[]{:S(2)}) copy-start(f32[3]{0:T(128)} %applied_ref.1) | copy-start | bytes 40
  21.6 0.6 %copy-start.6 = (f32[64,256]{1,0:T(8,128)}, f32[64,256]{1,0:T(8,128)S(1)}, u32[]{:S(2)}) copy-start(f32[64,256]{1,0:T(8,128)S(1)} %get-tuple-element.14.layer_ref) | copy-start | bytes 196612
  39.1 1.3 %copy-start.12 = (f32[16,256]{1,0:T(8,128)S(1)}, f32[16,256]{1,0:T(8,128)}, u32[]{:S(2)}) copy-start(f32[16,256]{1,0:T(8,128)} %get-tuple-element.22) | copy-start | bytes 49156

commit v2 on v1

v2 whole, which is shorter than its diff:
```python
import functools
import math

import jax
import jax.numpy as jnp
import numpy as np
from jax import lax
from jax.experimental import pallas as pl
from jax.experimental.pallas import tpu as pltpu
from jax.sharding import PartitionSpec as P
import ml_dtypes

NZ = 12
STEPS = 4
DAMPING = 0.5
TIME_STEP = 0.12
LANES = 128
SUB = 8
MESH = pl.DeviceIdType.MESH


def iota(shape, dim):
    return lax.broadcasted_iota(jnp.int32, shape, dim)


def sin_cos(x):
    turns = jnp.floor(x * (2.0 / math.pi) + 0.5)
    quadrant = turns.astype(jnp.int32)
    r = x - turns * 1.5703125
    r = r - turns * 4.837512969970703125e-4
    r = r - turns * 7.549789948768648e-8
    z = r * r
    sine = r + r * z * (-1.6666654611e-1 + z * (8.3321608736e-3 - z * 1.9515295891e-4))
    cosine = 1.0 - 0.5 * z + z * z * (
        4.166664568298827e-2 + z * (-1.388731625493765e-3 + z * 2.443315711809948e-5)
    )
    odd = (quadrant & 1) == 1
    s = jnp.where(odd, cosine, sine)
    c = jnp.where(odd, sine, cosine)
    s = jnp.where((quadrant & 2) == 2, -s, s)
    c = jnp.where(((quadrant + 1) & 2) == 2, -c, c)
    return s, c


def wrap(value, count):
    return jnp.where(value >= count, value - count, value)


def for_others(ngx, ngy, gx, gy, act):
    def row(i, first):
        other_x = wrap(gx + i, ngx)
        for j in range(first, ngy):
            act(other_x, wrap(gy + j, ngy))

    def turn(i, carry):
        row(i, 0)
        return carry

    row(0, 1)
    lax.fori_loop(1, ngx, turn, 0)


def split(values):
    high = values.astype(ml_dtypes.bfloat16)
    low = (values - high.astype(np.float64)).astype(ml_dtypes.bfloat16)
    return high, low


def wave_tables(ngx, ngy, width_x, width_y):
    total_x, total_y = width_x * ngx, width_y * ngy
    devices = ngx * ngy
    per_x, per_y = width_x // ngy, width_y // ngx
    x = np.arange(total_x)
    angle = 2.0 * np.pi / total_x * (np.outer(x, x) % total_x)
    both = np.stack([np.cos(angle), -np.sin(angle)], axis=1).reshape(total_x, 2, devices, per_x)
    table_x = both.transpose(0, 2, 1, 3).reshape(total_x, 2 * total_x)
    y = np.arange(total_y)
    angle = 2.0 * np.pi / total_y * (np.outer(y, y) % total_y)
    both = np.concatenate([np.cos(angle), np.sin(angle)], axis=1)
    table_y = np.zeros((devices, SUB, 2 * total_y))
    table_y[:, :per_y] = both.reshape(devices, per_y, 2 * total_y)
    return (*split(table_x), *split(table_y.reshape(devices * SUB, 2 * total_y)))


def two_parts(value):
    high = value.astype(jnp.bfloat16).astype(jnp.float32)
    return jnp.concatenate([high, value - high], axis=0).astype(jnp.bfloat16)


def product(value, high_ref, low_ref):
    rows = value.shape[0]
    parts = two_parts(value)
    big = jnp.dot(parts, high_ref[...], preferred_element_type=jnp.float32)
    head = -(-rows // 16) * 16
    small = jnp.dot(parts[:head], low_ref[...], preferred_element_type=jnp.float32)
    return (big[rows:] + small[:rows]) + big[:rows]


def main_kernel(
    ngx, ngy, p_hbm, a_hbm, g_hbm, xh_hbm, xl_hbm, yh_hbm, yl_hbm,
    stiff_ref, anis_ref, apol_ref, aazi_ref, applied_ref, moment_hbm, spectrum_ref,
    p_ref, a_ref, g_ref, xh, xl, yh, yl,
    rows_msg, cols_msg, corners_msg, rows_out, cols_out, corners_out,
    m_ref, w_ref, coef_ref, axis_ref, moment_ref, layer_ref, lines, message, held,
    load, send, recv, send_x, recv_x, send_y, recv_y,
):
    devices = ngx * ngy
    gx, gy = lax.axis_index("gx"), lax.axis_index("gy")
    down, up = wrap(gx + 1, ngx), wrap(gx + ngx - 1, ngx)
    right, left = wrap(gy + 1, ngy), wrap(gy + ngy - 1, ngy)
    around = [
        (up, gy), (down, gy), (gx, left), (gx, right),
        (up, left), (up, right), (down, left), (down, right),
    ]
    pairs = [
        (p_hbm, p_ref), (a_hbm, a_ref), (g_hbm, g_ref),
        (xh_hbm, xh), (xl_hbm, xl), (yh_hbm, yh), (yl_hbm, yl),
    ]
    loads = [pltpu.make_async_copy(s, t, load.at[k]) for k, (s, t) in enumerate(pairs)]
    for copy in loads[:3]:
        copy.start()
    barrier = pltpu.get_barrier_semaphore()

    def greet(other_x, other_y):
        pl.semaphore_signal(barrier, inc=1, device_id=(other_x, other_y), device_id_type=MESH)

    for_others(ngx, ngy, gx, gy, greet)
    for copy in loads[:3]:
        copy.wait()

    rows, columns = p_ref.shape
    half = columns // 2
    near = (slice(0, SUB), slice(rows - SUB, rows))
    side = (slice(0, LANES), slice(columns - LANES, columns))
    sub_low = iota((SUB, columns), 0) < 4
    for k in range(2):
        own = sub_low if k == 0 else jnp.logical_not(sub_low)
        g = g_ref[near[k], :].astype(jnp.float32)
        rows_msg[k, :, :columns] = jnp.where(
            own, p_ref[near[k], :], pltpu.roll(a_ref[near[k], :], 4, 0)
        )
        rows_msg[k, :, columns:] = jnp.where(
            own[:, :half], g[:, :half], pltpu.roll(g[:, half:], 4, 0)
        )
    lane_low = iota((rows, LANES), 1) < 64
    for k in range(2):
        own = lane_low if k == 0 else jnp.logical_not(lane_low)
        g = g_ref[:, side[k]].astype(jnp.float32)
        cols_msg[k, :rows] = jnp.where(own, p_ref[:, side[k]], pltpu.roll(a_ref[:, side[k]], 64, 1))
        cols_msg[k, rows:] = jnp.where(
            own[: rows // 2], g[: rows // 2], pltpu.roll(g[rows // 2 :], 64, 1)
        )
    tile_sub = iota((SUB, LANES), 0) < 4
    tile_lane = iota((SUB, LANES), 1) < 64
    for k in range(2):
        for j in range(2):
            own_sub = tile_sub if k == 0 else jnp.logical_not(tile_sub)
            own_lane = tile_lane if j == 0 else jnp.logical_not(tile_lane)
            g = g_ref[near[k], side[j]].astype(jnp.float32)
            corners_msg[2 * k + j] = jnp.where(
                own_sub,
                jnp.where(own_lane, p_ref[near[k], side[j]], pltpu.roll(a_ref[near[k], side[j]], 64, 1)),
                pltpu.roll(g, 4, 0),
            )
    pl.semaphore_wait(barrier, devices - 1)
    sources = [rows_msg.at[0], rows_msg.at[1], cols_msg.at[0], cols_msg.at[1]]
    sources += [corners_msg.at[k] for k in range(4)]
    targets = [rows_out.at[0], rows_out.at[1], cols_out.at[0], cols_out.at[1]]
    targets += [corners_out.at[k] for k in range(4)]
    copies = [
        pltpu.make_async_remote_copy(
            src_ref=sources[k], dst_ref=targets[k], send_sem=send.at[k], recv_sem=recv.at[k],
            device_id=around[k], device_id_type=MESH,
        )
        for k in range(8)
    ]
    for copy in copies:
        copy.start()
    for copy in loads[3:]:
        copy.start()

    strips, tiles = rows // SUB, columns // LANES
    lane = iota((SUB, LANES), 1)
    sub = iota((SUB, LANES), 0)
    sub_low, lane_low = sub < 4, lane < 64

    def raw(s, t):
        if s < strips and t < tiles:
            r, c = slice(s * SUB, s * SUB + SUB), slice(t * LANES, t * LANES + LANES)
            return p_ref[r, c], a_ref[r, c], g_ref[r, c]
        if s < strips:
            r = slice(s * SUB, s * SUB + SUB)
            k = (s * SUB) % (rows // 2) + rows
            rg = slice(k, k + SUB)
            fr, fl = cols_out[0, r, :], cols_out[1, r, :]
            gr, gl = cols_out[0, rg, :], cols_out[1, rg, :]
            p = jnp.where(lane_low, fr, fl)
            a = pltpu.roll(jnp.where(lane_low, fl, fr), 64, 1)
            if s * SUB < rows // 2:
                g = jnp.where(lane_low, gr, gl)
            else:
                g = pltpu.roll(jnp.where(lane_low, gl, gr), 64, 1)
        elif t < tiles:
            c = slice(t * LANES, t * LANES + LANES)
            k = (t * LANES) % half + columns
            cg = slice(k, k + LANES)
            fn, fp = rows_out[0, :, c], rows_out[1, :, c]
            gn, gp = rows_out[0, :, cg], rows_out[1, :, cg]
            p = jnp.where(sub_low, fn, fp)
            a = pltpu.roll(jnp.where(sub_low, fp, fn), 4, 0)
            if t * LANES < half:
                g = jnp.where(sub_low, gn, gp)
            else:
                g = pltpu.roll(jnp.where(sub_low, gp, gn), 4, 0)
        else:
            q = [corners_out[k] for k in range(4)]
            p = jnp.where(sub_low, jnp.where(lane_low, q[0], q[1]), jnp.where(lane_low, q[2], q[3]))
            a = jnp.where(sub_low, jnp.where(lane_low, q[1], q[0]), jnp.where(lane_low, q[3], q[2]))
            a = pltpu.roll(a, 64, 1)
            g = jnp.where(sub_low, jnp.where(lane_low, q[2], q[3]), jnp.where(lane_low, q[0], q[1]))
            g = pltpu.roll(g, 4, 0)
        return p, a, g.astype(jnp.int32)

    def store(ref, lead, s, t, value):
        ref[(*lead, t, slice(SUB + s * SUB, 2 * SUB + s * SUB), slice(None))] = value
        if s == 0:
            k = SUB * (strips + 2)
            ref[(*lead, t, slice(k, k + SUB), slice(None))] = value
        if s == strips:
            ref[(*lead, t, slice(0, SUB), slice(None))] = value

    def rows_of(ref, lead, s, t, shift=0):
        k = SUB + s * SUB + shift
        return ref[(*lead, t, slice(k, k + SUB), slice(None))]

    sp, cp = sin_cos(apol_ref[...])
    sa, ca = sin_cos(aazi_ref[...])
    root = jnp.sqrt(anis_ref[...])
    tables = [stiff_ref[...], root * sp * ca, root * sp * sa, root * cp]
    pages = [
        [jnp.broadcast_to(table[:, k : k + LANES], (SUB, LANES)) for k in range(0, table.shape[1], LANES)]
        for table in tables
    ]

    def prepare(s, t):
        p, a, g = raw(s, t)
        sp, cp = sin_cos(p)
        sa, ca = sin_cos(a)
        for c, value in enumerate((sp * ca, sp * sa, cp)):
            store(m_ref, (0, c), s, t, value)
        place = g & (LANES - 1)
        page = g >> 7
        found = []
        for table in pages:
            value = jnp.take_along_axis(table[0], place, axis=1, mode="promise_in_bounds")
            for k in range(1, len(table)):
                other = jnp.take_along_axis(table[k], place, axis=1, mode="promise_in_bounds")
                value = jnp.where(page == k, other, value)
            found.append(value)
        store(w_ref, (), s, t, found[0])
        for c in range(3):
            axis_ref[c, t, s * SUB : s * SUB + SUB, :] = found[1 + c]

    for s in range(strips):
        for t in range(tiles):
            prepare(s, t)
    for copy in copies:
        copy.wait()
    for s in range(strips + 1):
        for t in range(tiles + 1):
            if s == strips or t == tiles:
                prepare(s, t)

    count = tiles + 1

    def shifter(values, shift):
        turned = {}

        def turn(t):
            t = t % count
            if t not in turned:
                turned[t] = pltpu.roll(values[t], (-shift) % LANES, 1)
            return turned[t]

        def at(t):
            if shift > 0:
                return jnp.where(lane < LANES - shift, turn(t), turn(t + 1))
            return jnp.where(lane >= -shift, turn(t), turn(t - 1))

        return at

    def couple(p, q):
        return 2.0 * p * q / (p + q)

    for s in range(strips + 1):
        here = [rows_of(w_ref, (), s, t) for t in range(count)]
        plus_y = shifter(here, NZ)
        plus_z = shifter(here, 1)
        y_link = [couple(here[t], plus_y(t)) for t in range(count)]
        z_link = []
        for t in range(count):
            spot = t * LANES + lane
            if t == tiles:
                spot = jnp.where(lane_low, spot, spot - count * LANES + NZ * LANES)
            level = spot - NZ * ((spot * 43691) >> 19)
            z_link.append(jnp.where(level < NZ - 1, couple(here[t], plus_z(t)), 0.0))
        y_back = shifter(y_link, -NZ)
        z_back = shifter(z_link, -1)
        for t in range(count):
            links = [
                couple(here[t], rows_of(w_ref, (), s, t, 1)),
                couple(here[t], rows_of(w_ref, (), s, t, -1)),
                y_link[t],
                y_back(t),
                z_link[t],
                z_back(t),
            ]
            total = links[0] + links[1] + links[2] + links[3] + links[4] + links[5]
            for k, value in enumerate(links + [total]):
                coef_ref[k, t, s * SUB : s * SUB + SUB, :] = value

    applied = [applied_ref[c] for c in range(3)]
    factor = TIME_STEP / (1.0 + DAMPING * DAMPING)

    def one_step(index, carry):
        now = lax.rem(index, 2)
        later = 1 - now
        for s in range(strips + 1):
            here = [[rows_of(m_ref, (now, c), s, t) for t in range(count)] for c in range(3)]
            shifts = [[shifter(here[c], k) for k in (NZ, -NZ, 1, -1)] for c in range(3)]
            for t in range(count):
                spot = (t, slice(s * SUB, s * SUB + SUB), slice(None))
                link = [coef_ref[(k, *spot)] for k in range(7)]
                easy = [axis_ref[(c, *spot)] for c in range(3)]
                m = [here[c][t] for c in range(3)]
                project = easy[0] * m[0] + easy[1] * m[1] + easy[2] * m[2]
                h = []
                for c in range(3):
                    value = link[0] * rows_of(m_ref, (now, c), s, t, 1)
                    value = value + link[1] * rows_of(m_ref, (now, c), s, t, -1)
                    for k in range(4):
                        value = value + link[2 + k] * shifts[c][k](t)
                    value = value - link[6] * m[c]
                    h.append(value + project * easy[c] + applied[c])

                def cross(f, g):
                    return [
                        f[1] * g[2] - f[2] * g[1],
                        f[2] * g[0] - f[0] * g[2],
                        f[0] * g[1] - f[1] * g[0],
                    ]

                torque = cross(m, h)
                damped = cross(m, torque)
                moved = [
                    m[c] - (factor * torque[c] + (factor * DAMPING) * damped[c]) for c in range(3)
                ]
                size = moved[0] * moved[0] + moved[1] * moved[1] + moved[2] * moved[2]
                inverse = lax.rsqrt(size)
                for c in range(3):
                    store(m_ref, (later, c), s, t, moved[c] * inverse)
        return carry

    lax.fori_loop(0, STEPS, one_step, 0)

    last = STEPS % 2
    width_y = columns // NZ
    per = width_y // ngx
    row = iota((ngx * SUB, columns), 0)
    column = iota((ngx * SUB, columns), 1)
    cell = (row // SUB) * per + row % SUB
    inside = (column >= cell * NZ) & (column < cell * NZ + NZ) & (row % SUB < per)
    chooser = jnp.where(inside, 1.0, 0.0).astype(jnp.bfloat16)
    out_copy = pltpu.make_async_copy(moment_ref, moment_hbm, load.at[7])
    for c in range(3):
        for t in range(tiles):
            moment_ref[c, :, t * LANES : t * LANES + LANES] = m_ref[last, c, t, SUB : SUB + rows, :]
        whole = moment_ref[c]
        high = whole.astype(jnp.bfloat16)
        low = (whole - high.astype(jnp.float32)).astype(jnp.bfloat16)
        sums = sum(
            lax.dot_general(
                chooser, part, (((1,), (1,)), ((), ())), preferred_element_type=jnp.float32
            )
            for part in (low, high)
        )
        layer_ref[:, c * rows : c * rows + rows] = sums * (1.0 / math.sqrt(NZ))
    layer_ref[:, 3 * rows :] = jnp.zeros((ngx * SUB, rows), jnp.float32)

    def eight(index):
        return pl.ds(pl.multiple_of(index * SUB, SUB), SUB)

    mine = eight(gx)
    for k in range(1, ngx):
        other = wrap(gx + k, ngx)
        pltpu.make_async_remote_copy(
            src_ref=layer_ref.at[eight(other)], dst_ref=lines.at[mine],
            send_sem=send_x, recv_sem=recv_x, device_id=(other, gy), device_id_type=MESH,
        ).start()
    out_copy.start()
    lines[mine, :] = layer_ref[mine, :]
    rest = pl.ds(0, (ngx - 1) * SUB)
    pltpu.make_async_remote_copy(
        src_ref=layer_ref.at[rest], dst_ref=lines.at[rest], send_sem=send_x, recv_sem=recv_x,
        device_id=(wrap(gx + 1, ngx), gy), device_id_type=MESH,
    ).wait()
    loads[3].wait()
    loads[4].wait()
    whole = jnp.concatenate(
        [
            jnp.concatenate(
                [lines[s * SUB : s * SUB + SUB, c * rows : c * rows + rows] for s in range(ngx)],
                axis=1,
            )
            for c in range(3)
        ],
        axis=0,
    )
    waves = product(whole, xh, xl)
    per_x = rows // ngy
    wide = 2 * per_x
    blank = jnp.zeros((SUB, LANES - 3 * wide), jnp.float32)
    for d in range(devices):
        pieces = [waves[c * SUB : c * SUB + SUB, d * wide : d * wide + wide] for c in range(3)]
        message[d] = jnp.concatenate(pieces + [blank], axis=1)

    slot = gy * ngx + gx

    def give(other_x, other_y):
        pltpu.make_async_remote_copy(
            src_ref=message.at[other_x * ngy + other_y], dst_ref=held.at[slot],
            send_sem=send_y, recv_sem=recv_y, device_id=(other_x, other_y), device_id_type=MESH,
        ).start()

    for_others(ngx, ngy, gx, gy, give)
    held[slot] = message[gx * ngy + gy]
    loads[5].wait()
    loads[6].wait()
    rest = pl.ds(0, devices - 1)
    pltpu.make_async_remote_copy(
        src_ref=message.at[rest], dst_ref=held.at[rest], send_sem=send_y, recv_sem=recv_y,
        device_id=(wrap(gx + 1, ngx), gy), device_id_type=MESH,
    ).wait()
    table = held[...].reshape(devices * SUB, LANES).T
    total_y = yh.shape[1] // 2
    scale = 1.0 / math.sqrt(ngx * rows * total_y)
    spectrum = product(table, yh, yl) * scale
    for c in range(3):
        re = spectrum[c * wide : c * wide + per_x]
        im = spectrum[c * wide + per_x : c * wide + wide]
        spectrum_ref[c] = re[:, :total_y] + im[:, total_y:]
        spectrum_ref[3 + c] = im[:, :total_y] - re[:, total_y:]
    out_copy.wait()


def main(ngx, ngy, polar, azimuth, grains, tables, applied):
    rows, columns = polar.shape
    width_y = columns // NZ
    devices = ngx * ngy
    vmem, hbm = pl.BlockSpec(memory_space=pltpu.VMEM), pl.BlockSpec(memory_space=pl.ANY)
    strips, tiles = rows // SUB + 1, columns // LANES + 1
    waves = wave_tables(ngx, ngy, rows, width_y)
    messages = [(2, SUB, columns + columns // 2), (2, rows + rows // 2, LANES), (4, SUB, LANES)]
    floats = messages + messages + [
        (2, 3, tiles, SUB * (strips + 2), LANES),
        (tiles, SUB * (strips + 2), LANES),
        (7, tiles, SUB * strips, LANES),
        (3, tiles, SUB * strips, LANES),
        (3, rows, columns),
        (ngx * SUB, 4 * rows),
        (ngx * SUB, 4 * rows),
        (devices, SUB, LANES),
        (devices, SUB, LANES),
    ]
    dma = pltpu.SemaphoreType.DMA
    return pl.pallas_call(
        functools.partial(main_kernel, ngx, ngy),
        out_shape=[
            jax.ShapeDtypeStruct((3, rows, columns), jnp.float32),
            jax.ShapeDtypeStruct((6, rows // ngy, width_y * ngy), jnp.float32),
        ],
        in_specs=[hbm] * 7 + [vmem] * 4 + [pl.BlockSpec(memory_space=pltpu.SMEM)],
        out_specs=[hbm, vmem],
        scratch_shapes=[pltpu.VMEM(polar.shape, jnp.float32)] * 2
        + [pltpu.VMEM(polar.shape, jnp.int32)]
        + [pltpu.VMEM(t.shape, jnp.bfloat16) for t in waves]
        + [pltpu.VMEM(shape, jnp.float32) for shape in floats]
        + [dma((8,)), dma((8,)), dma((8,)), dma(()), dma(()), dma(()), dma(())],
        compiler_params=pltpu.CompilerParams(
            collective_id=0, has_side_effects=True, vmem_limit_bytes=60 * 2**20
        ),
        name="main",
    )(polar, azimuth, grains, *[jnp.asarray(t) for t in waves], *tables, applied)


def finish_kernel(ngx, ngy, spectrum_ref, moment_in, moment_out, flip_ref, non_ref, sem):
    copies = [
        pltpu.make_async_copy(moment_in.at[c], moment_out.at[c], sem.at[c]) for c in range(3)
    ]
    for copy in copies:
        copy.start()
    me = lax.axis_index("gx") * ngy + lax.axis_index("gy")
    per_x, total_y = flip_ref.shape
    total_x = per_x * ngx * ngy
    counter_x = me * per_x + iota((per_x, total_y), 0)
    counter_y = iota((per_x, total_y), 1)
    wave_x = jnp.where(counter_x < total_x // 2, counter_x, counter_x - total_x).astype(jnp.float32)
    wave_y = jnp.where(counter_y < total_y // 2, counter_y, counter_y - total_y).astype(jnp.float32)
    squared = wave_x * wave_x + wave_y * wave_y
    inverse = 1.0 / jnp.sqrt(jnp.maximum(squared, 1.0))
    beam_stop = jnp.where(squared > 0.5, 1.0, 0.0)
    unit_x, unit_y = wave_x * inverse, wave_y * inverse
    real = [spectrum_ref[c] for c in range(3)]
    imag = [spectrum_ref[3 + c] for c in range(3)]
    flip = jnp.zeros_like(squared)
    non = jnp.zeros_like(squared)
    for part in (real, imag):
        along = unit_x * part[0] + unit_y * part[1]
        first = part[0] - unit_x * along
        second = part[1] - unit_y * along
        non = non + first * first
        flip = flip + second * second + part[2] * part[2]
    flip_ref[...] = flip * beam_stop
    non_ref[...] = non * beam_stop
    for copy in copies:
        copy.wait()


def finish(ngx, ngy, spectrum, moment):
    vmem, hbm = pl.BlockSpec(memory_space=pltpu.VMEM), pl.BlockSpec(memory_space=pl.ANY)
    out = jax.ShapeDtypeStruct(spectrum.shape[1:], jnp.float32)
    return pl.pallas_call(
        functools.partial(finish_kernel, ngx, ngy),
        out_shape=[jax.ShapeDtypeStruct(moment.shape, jnp.float32), out, out],
        in_specs=[vmem, hbm],
        out_specs=[hbm, vmem, vmem],
        scratch_shapes=[pltpu.SemaphoreType.DMA((3,))],
        compiler_params=pltpu.CompilerParams(vmem_limit_bytes=60 * 2**20),
        name="finish",
    )(spectrum, moment)


def solution(mesh):
    ngx, ngy = mesh.shape["gx"], mesh.shape["gy"]

    def shards(polar, azimuth, grains, stiffness, anisotropy, axis_polar, axis_azimuth, applied):
        tables = [t.reshape(1, -1) for t in (stiffness, anisotropy, axis_polar, axis_azimuth)]
        moment, spectrum = main(ngx, ngy, polar, azimuth, grains, tables, applied)
        return tuple(finish(ngx, ngy, spectrum, moment))

    in_specs = (P("gx", "gy"), P("gx", "gy"), P("gx", "gy"), P(), P(), P(), P(), P())
    out_specs = (P(None, "gx", "gy"), P(("gx", "gy"), None), P(("gx", "gy"), None))
    return jax.shard_map(shards, mesh=mesh, in_specs=in_specs, out_specs=out_specs, check_vma=False)
```

time: 41.4 us -> 49.6 us (1.20)
  Pallas kernels: 34.3 us -> 48.8 us
  local copies, waits for them, and re-layouts: 5.96 us -> 0 us
    pallas_call x3 -> x2, Pallas kernels: 34.3 us -> 48.8 us  [the longest x1 28.3 us: main(): pl.pallas_call(functools.partial(main_kernel, ngx, ngy), out_shape=[jax.S...]
    unnamed x28 -> x0, local copies, waits for them, and re-layouts: 5.96 us -> none
where the time goes in v2:
time: 49.6 us; the launch traced here: 49.4 us
  Pallas kernels  48.8 us (98%)
  between operations  0.64 us (1%)
    pallas_call x1, Pallas kernels, main(): pl.pallas_call(functools.partial(main_kernel, ngx, ngy), out_shape=[jax.S...  28.3 us
    pallas_call x1, Pallas kernels, finish(): pl.pallas_call(functools.partial(finish_kernel, ngx, ngy), out_shape=[jax...  20.5 us

profile of v2, /device:TPU:0, one launch (start us, length us, event | category | flops | bytes accessed | tf_op | source)
XLA Modules:
  0.0 49.4 jit_solution(8406218622650390059)
XLA Ops:
  0.6 28.3 %main.1 = (f32[3,64,768]{2,1,0:T(8,128)}, f32[6,16,256]{2,1,0:T(8,128)}) custom-call(f32[64,768]{1,0:T(8,128)} %p_hbm.1, f32[64,768]{1,0:T(8,128)} %a_hbm.1, s32[64,768]{1,0:T(8,128)} %g_hbm.1, bf16[512,1024]{1,0:T(8,128)(2,1)} %constant.8.clone.xh_hbm, bf16[512,1024]{1,0:T(8,128)(2,1)} %constant.9.clone.xl_hbm, bf16[256,512]{1,0:T(8,128)(2,1)} %constant.10.clone.yh_hbm, ...), custom_call_target="tpu_custom_call" | custom-call | tf_op jit(solution)/shard_map/main/pallas_call | solution.py:476
  28.9 20.5 %finish.1 = (f32[3,64,768]{2,1,0:T(8,128)}, f32[16,256]{1,0:T(8,128)}, f32[16,256]{1,0:T(8,128)}) custom-call(f32[6,16,256]{2,1,0:T(8,128)} %get-tuple-element.5.spectrum_ref, f32[3,64,768]{2,1,0:T(8,128)} %get-tuple-element.6.moment_in), custom_call_target="tpu_custom_call" | custom-call | tf_op jit(solution)/shard_map/finish/pallas_call | solution.py:532

commit v3 on v2

--- a/solution.py
+++ b/solution.py
@@ -98,10 +98,10 @@
 
 def main_kernel(
     ngx, ngy, p_hbm, a_hbm, g_hbm, xh_hbm, xl_hbm, yh_hbm, yl_hbm,
-    stiff_ref, anis_ref, apol_ref, aazi_ref, applied_ref, moment_hbm, spectrum_ref,
-    p_ref, a_ref, g_ref, xh, xl, yh, yl,
+    stiff_hbm, anis_hbm, apol_hbm, aazi_hbm, applied_ref, moment_ref, spectrum_ref,
+    p_ref, a_ref, g_ref, xh, xl, yh, yl, stiff_ref, anis_ref, apol_ref, aazi_ref,
     rows_msg, cols_msg, corners_msg, rows_out, cols_out, corners_out,
-    m_ref, w_ref, coef_ref, axis_ref, moment_ref, layer_ref, lines, message, held,
+    m_ref, w_ref, coef_ref, axis_ref, layer_ref, lines, message, held,
     load, send, recv, send_x, recv_x, send_y, recv_y,
 ):
     devices = ngx * ngy
@@ -115,9 +115,10 @@
     pairs = [
         (p_hbm, p_ref), (a_hbm, a_ref), (g_hbm, g_ref),
         (xh_hbm, xh), (xl_hbm, xl), (yh_hbm, yh), (yl_hbm, yl),
+        (stiff_hbm, stiff_ref), (anis_hbm, anis_ref), (apol_hbm, apol_ref), (aazi_hbm, aazi_ref),
     ]
     loads = [pltpu.make_async_copy(s, t, load.at[k]) for k, (s, t) in enumerate(pairs)]
-    for copy in loads[:3]:
+    for copy in loads[:3] + loads[7:]:
         copy.start()
     barrier = pltpu.get_barrier_semaphore()
 
@@ -176,8 +177,10 @@
     ]
     for copy in copies:
         copy.start()
-    for copy in loads[3:]:
+    for copy in loads[3:7]:
         copy.start()
+    for copy in loads[7:]:
+        copy.wait()
 
     strips, tiles = rows // SUB, columns // LANES
     lane = iota((SUB, LANES), 1)
@@ -322,13 +325,11 @@
     applied = [applied_ref[c] for c in range(3)]
     factor = TIME_STEP / (1.0 + DAMPING * DAMPING)
 
-    def one_step(index, carry):
-        now = lax.rem(index, 2)
-        later = 1 - now
-        for s in range(strips + 1):
+    def one_step(now, put, strip_count, tile_count):
+        for s in range(strip_count):
             here = [[rows_of(m_ref, (now, c), s, t) for t in range(count)] for c in range(3)]
             shifts = [[shifter(here[c], k) for k in (NZ, -NZ, 1, -1)] for c in range(3)]
-            for t in range(count):
+            for t in range(tile_count):
                 spot = (t, slice(s * SUB, s * SUB + SUB), slice(None))
                 link = [coef_ref[(k, *spot)] for k in range(7)]
                 easy = [axis_ref[(c, *spot)] for c in range(3)]
@@ -358,12 +359,23 @@
                 size = moved[0] * moved[0] + moved[1] * moved[1] + moved[2] * moved[2]
                 inverse = lax.rsqrt(size)
                 for c in range(3):
-                    store(m_ref, (later, c), s, t, moved[c] * inverse)
+                    put(c, s, t, moved[c] * inverse)
+
+    def early_step(index, carry):
+        now = lax.rem(index, 2)
+
+        def put(c, s, t, value):
+            store(m_ref, (1 - now, c), s, t, value)
+
+        one_step(now, put, strips + 1, count)
         return carry
 
-    lax.fori_loop(0, STEPS, one_step, 0)
-
-    last = STEPS % 2
+    def put_moment(c, s, t, value):
+        moment_ref[c, s * SUB : s * SUB + SUB, t * LANES : t * LANES + LANES] = value
+
+    lax.fori_loop(0, STEPS - 1, early_step, 0)
+    one_step((STEPS - 1) % 2, put_moment, strips, tiles)
+
     width_y = columns // NZ
     per = width_y // ngx
     row = iota((ngx * SUB, columns), 0)
@@ -371,10 +383,7 @@
     cell = (row // SUB) * per + row % SUB
     inside = (column >= cell * NZ) & (column < cell * NZ + NZ) & (row % SUB < per)
     chooser = jnp.where(inside, 1.0, 0.0).astype(jnp.bfloat16)
-    out_copy = pltpu.make_async_copy(moment_ref, moment_hbm, load.at[7])
     for c in range(3):
-        for t in range(tiles):
-            moment_ref[c, :, t * LANES : t * LANES + LANES] = m_ref[last, c, t, SUB : SUB + rows, :]
         whole = moment_ref[c]
         high = whole.astype(jnp.bfloat16)
         low = (whole - high.astype(jnp.float32)).astype(jnp.bfloat16)
@@ -397,7 +406,6 @@
             src_ref=layer_ref.at[eight(other)], dst_ref=lines.at[mine],
             send_sem=send_x, recv_sem=recv_x, device_id=(other, gy), device_id_type=MESH,
         ).start()
-    out_copy.start()
     lines[mine, :] = layer_ref[mine, :]
     rest = pl.ds(0, (ngx - 1) * SUB)
     pltpu.make_async_remote_copy(
@@ -450,14 +458,13 @@
         im = spectrum[c * wide + per_x : c * wide + wide]
         spectrum_ref[c] = re[:, :total_y] + im[:, total_y:]
         spectrum_ref[3 + c] = im[:, :total_y] - re[:, total_y:]
-    out_copy.wait()
 
 
 def main(ngx, ngy, polar, azimuth, grains, tables, applied):
     rows, columns = polar.shape
     width_y = columns // NZ
     devices = ngx * ngy
-    vmem, hbm = pl.BlockSpec(memory_space=pltpu.VMEM), pl.BlockSpec(memory_space=pl.ANY)
+    vmem, hbm = pl.BlockSpec(memory_space=pltpu.VMEM), pl.BlockSpec(memory_space=pltpu.HBM)
     strips, tiles = rows // SUB + 1, columns // LANES + 1
     waves = wave_tables(ngx, ngy, rows, width_y)
     messages = [(2, SUB, columns + columns // 2), (2, rows + rows // 2, LANES), (4, SUB, LANES)]
@@ -466,37 +473,48 @@
         (tiles, SUB * (strips + 2), LANES),
         (7, tiles, SUB * strips, LANES),
         (3, tiles, SUB * strips, LANES),
-        (3, rows, columns),
         (ngx * SUB, 4 * rows),
         (ngx * SUB, 4 * rows),
         (devices, SUB, LANES),
         (devices, SUB, LANES),
     ]
     dma = pltpu.SemaphoreType.DMA
+
+    def in_hbm(value):
+        return pltpu.with_memory_space_constraint(jnp.asarray(value), pltpu.HBM)
+
+    held_bytes = sum(2 * t.size for t in waves) + sum(4 * math.prod(f) for f in floats)
+    room = min(60, 10 + held_bytes // 2**20)
     return pl.pallas_call(
         functools.partial(main_kernel, ngx, ngy),
         out_shape=[
             jax.ShapeDtypeStruct((3, rows, columns), jnp.float32),
             jax.ShapeDtypeStruct((6, rows // ngy, width_y * ngy), jnp.float32),
         ],
-        in_specs=[hbm] * 7 + [vmem] * 4 + [pl.BlockSpec(memory_space=pltpu.SMEM)],
-        out_specs=[hbm, vmem],
+        in_specs=[hbm] * 11 + [pl.BlockSpec(memory_space=pltpu.SMEM)],
+        out_specs=[vmem, vmem],
         scratch_shapes=[pltpu.VMEM(polar.shape, jnp.float32)] * 2
         + [pltpu.VMEM(polar.shape, jnp.int32)]
         + [pltpu.VMEM(t.shape, jnp.bfloat16) for t in waves]
+        + [pltpu.VMEM(t.shape, jnp.float32) for t in tables]
         + [pltpu.VMEM(shape, jnp.float32) for shape in floats]
-        + [dma((8,)), dma((8,)), dma((8,)), dma(()), dma(()), dma(()), dma(())],
+        + [dma((11,)), dma((8,)), dma((8,)), dma(()), dma(()), dma(()), dma(())],
         compiler_params=pltpu.CompilerParams(
-            collective_id=0, has_side_effects=True, vmem_limit_bytes=60 * 2**20
+            collective_id=0, has_side_effects=True, vmem_limit_bytes=room * 2**20
         ),
         name="main",
-    )(polar, azimuth, grains, *[jnp.asarray(t) for t in waves], *tables, applied)
+    )(*[in_hbm(t) for t in (polar, azimuth, grains, *waves, *tables, applied)])
 
 
 def finish_kernel(ngx, ngy, spectrum_ref, moment_in, moment_out, flip_ref, non_ref, sem):
-    copies = [
-        pltpu.make_async_copy(moment_in.at[c], moment_out.at[c], sem.at[c]) for c in range(3)
-    ]
+    rows = moment_in.shape[1]
+    copies = []
+    for c in range(3):
+        for k in range(4):
+            part = (c, pl.ds(k * (rows // 4), rows // 4))
+            copies.append(
+                pltpu.make_async_copy(moment_in.at[part], moment_out.at[part], sem.at[4 * c + k])
+            )
     for copy in copies:
         copy.start()
     me = lax.axis_index("gx") * ngy + lax.axis_index("gy")
@@ -527,15 +545,15 @@
 
 
 def finish(ngx, ngy, spectrum, moment):
-    vmem, hbm = pl.BlockSpec(memory_space=pltpu.VMEM), pl.BlockSpec(memory_space=pl.ANY)
+    vmem, hbm = pl.BlockSpec(memory_space=pltpu.VMEM), pl.BlockSpec(memory_space=pltpu.HBM)
     out = jax.ShapeDtypeStruct(spectrum.shape[1:], jnp.float32)
     return pl.pallas_call(
         functools.partial(finish_kernel, ngx, ngy),
         out_shape=[jax.ShapeDtypeStruct(moment.shape, jnp.float32), out, out],
-        in_specs=[vmem, hbm],
+        in_specs=[vmem, vmem],
         out_specs=[hbm, vmem, vmem],
-        scratch_shapes=[pltpu.SemaphoreType.DMA((3,))],
-        compiler_params=pltpu.CompilerParams(vmem_limit_bytes=60 * 2**20),
+        scratch_shapes=[pltpu.SemaphoreType.DMA((12,))],
+        compiler_params=pltpu.CompilerParams(vmem_limit_bytes=8 * 2**20),
         name="finish",
     )(spectrum, moment)
 

time: 49.6 us -> 29.6 us (0.60)
  Pallas kernels: 48.8 us -> 28.8 us
    pallas_call x1, Pallas kernels: 20.5 us -> 1.51 us  [finish(): pl.pallas_call(functools.partial(finish_kernel, ngx, ngy), out_shape=[jax...]
    pallas_call x1, Pallas kernels: 28.3 us -> 27.3 us  [main(): pl.pallas_call(functools.partial(main_kernel, ngx, ngy), out_shape=[jax.S...]
where the time goes in v3:
time: 29.6 us; the launch traced here: 29.5 us
  Pallas kernels  28.8 us (97%)
  between operations  0.64 us (2%)
    pallas_call x1, Pallas kernels, main(): pl.pallas_call(functools.partial(main_kernel, ngx, ngy), out_shape=[jax.S...  27.3 us
    pallas_call x1, Pallas kernels, finish(): pl.pallas_call(functools.partial(finish_kernel, ngx, ngy), out_shape=[jax...  1.51 us

profile of v3, /device:TPU:0, one launch (start us, length us, event | category | flops | bytes accessed | tf_op | source)
XLA Modules:
  0.0 29.5 jit_solution(15762523674329313853)
XLA Ops:
  0.6 27.3 %main.1 = (f32[3,64,768]{2,1,0:T(8,128)S(1)}, f32[6,16,256]{2,1,0:T(8,128)S(1)}) custom-call(f32[64,768]{1,0:T(8,128)} %p_hbm.1, f32[64,768]{1,0:T(8,128)} %a_hbm.1, s32[64,768]{1,0:T(8,128)} %g_hbm.1, bf16[512,1024]{1,0:T(8,128)(2,1)} %constant.8.clone.xh_hbm, bf16[512,1024]{1,0:T(8,128)(2,1)} %constant.9.clone.xl_hbm, ...), custom_call_target="tpu_custom_call" | custom-call | tf_op jit(solution)/shard_map/main/pallas_call | solution.py:488
  28.0 1.5 %finish.1 = (f32[3,64,768]{2,1,0:T(8,128)}, f32[16,256]{1,0:T(8,128)}, f32[16,256]{1,0:T(8,128)}) custom-call(f32[6,16,256]{2,1,0:T(8,128)S(1)} %get-tuple-element.5.spectrum_ref, f32[3,64,768]{2,1,0:T(8,128)S(1)} %get-tuple-element.6.moment_in), custom_call_target="tpu_custom_call" | custom-call | tf_op jit(solution)/shard_map/finish/pallas_call | solution.py:550

commit v4 on v3

--- a/solution.py
+++ b/solution.py
@@ -87,12 +87,11 @@
     return jnp.concatenate([high, value - high], axis=0).astype(jnp.bfloat16)
 
 
-def product(value, high_ref, low_ref):
-    rows = value.shape[0]
-    parts = two_parts(value)
-    big = jnp.dot(parts, high_ref[...], preferred_element_type=jnp.float32)
+def product(parts, high, low):
+    rows = parts.shape[0] // 2
+    big = jnp.dot(parts, high, preferred_element_type=jnp.float32)
     head = -(-rows // 16) * 16
-    small = jnp.dot(parts[:head], low_ref[...], preferred_element_type=jnp.float32)
+    small = jnp.dot(parts[:head], low, preferred_element_type=jnp.float32)
     return (big[rows:] + small[:rows]) + big[:rows]
 
 
@@ -424,23 +423,27 @@
         ],
         axis=0,
     )
-    waves = product(whole, xh, xl)
     per_x = rows // ngy
     wide = 2 * per_x
     blank = jnp.zeros((SUB, LANES - 3 * wide), jnp.float32)
-    for d in range(devices):
-        pieces = [waves[c * SUB : c * SUB + SUB, d * wide : d * wide + wide] for c in range(3)]
-        message[d] = jnp.concatenate(pieces + [blank], axis=1)
-
     slot = gy * ngx + gx
 
-    def give(other_x, other_y):
-        pltpu.make_async_remote_copy(
-            src_ref=message.at[other_x * ngy + other_y], dst_ref=held.at[slot],
-            send_sem=send_y, recv_sem=recv_y, device_id=(other_x, other_y), device_id_type=MESH,
-        ).start()
-
-    for_others(ngx, ngy, gx, gy, give)
+    parts = two_parts(whole)
+    for k in [*range(1, ngx), 0]:
+        other_x = wrap(gx + k, ngx)
+        lanes = pl.ds(pl.multiple_of(other_x * (wide * ngy), LANES), wide * ngy)
+        chunk = product(parts, xh[:, lanes], xl[:, lanes])
+        for j in range(ngy):
+            pieces = [chunk[c * SUB : c * SUB + SUB, j * wide : j * wide + wide] for c in range(3)]
+            message[other_x * ngy + j] = jnp.concatenate(pieces + [blank], axis=1)
+        for j in range(0 if k else 1, ngy):
+            other_y = wrap(gy + j, ngy)
+            pltpu.make_async_remote_copy(
+                src_ref=message.at[other_x * ngy + other_y], dst_ref=held.at[slot],
+                send_sem=send_y, recv_sem=recv_y, device_id=(other_x, other_y),
+                device_id_type=MESH,
+            ).start()
+
     held[slot] = message[gx * ngy + gy]
     loads[5].wait()
     loads[6].wait()
@@ -452,7 +455,7 @@
     table = held[...].reshape(devices * SUB, LANES).T
     total_y = yh.shape[1] // 2
     scale = 1.0 / math.sqrt(ngx * rows * total_y)
-    spectrum = product(table, yh, yl) * scale
+    spectrum = product(two_parts(table), yh[...], yl[...]) * scale
     for c in range(3):
         re = spectrum[c * wide : c * wide + per_x]
         im = spectrum[c * wide + per_x : c * wide + wide]

time: 29.6 us -> 29.5 us (level)
  no operation moved by 1% of the time
where the time goes in v4:
time: 29.5 us; the launch traced here: 29.3 us
  Pallas kernels  28.7 us (97%)
  between operations  0.64 us (2%)
    pallas_call x1, Pallas kernels, main(): pl.pallas_call(functools.partial(main_kernel, ngx, ngy), out_shape=[jax.S...  27.2 us
    pallas_call x1, Pallas kernels, finish(): pl.pallas_call(functools.partial(finish_kernel, ngx, ngy), out_shape=[jax...  1.51 us

profile of v4, /device:TPU:0, one launch (start us, length us, event | category | flops | bytes accessed | tf_op | source)
XLA Modules:
  0.0 29.3 jit_solution(16492524077182040741)
XLA Ops:
  0.6 27.2 %main.1 = (f32[3,64,768]{2,1,0:T(8,128)S(1)}, f32[6,16,256]{2,1,0:T(8,128)S(1)}) custom-call(f32[64,768]{1,0:T(8,128)} %p_hbm.1, f32[64,768]{1,0:T(8,128)} %a_hbm.1, s32[64,768]{1,0:T(8,128)} %g_hbm.1, bf16[512,1024]{1,0:T(8,128)(2,1)} %constant.8.clone.xh_hbm, bf16[512,1024]{1,0:T(8,128)(2,1)} %constant.9.clone.xl_hbm, ...), custom_call_target="tpu_custom_call" | custom-call | tf_op jit(solution)/shard_map/main/pallas_call | solution.py:491
  27.8 1.5 %finish.1 = (f32[3,64,768]{2,1,0:T(8,128)}, f32[16,256]{1,0:T(8,128)}, f32[16,256]{1,0:T(8,128)}) custom-call(f32[6,16,256]{2,1,0:T(8,128)S(1)} %get-tuple-element.5.spectrum_ref, f32[3,64,768]{2,1,0:T(8,128)S(1)} %get-tuple-element.6.moment_in), custom_call_target="tpu_custom_call" | custom-call | tf_op jit(solution)/shard_map/finish/pallas_call | solution.py:553
